TPU v7x, 128 devices: a whole 4x4x4 slice. The times are simulated.
128 devices in a mesh: section: 4 (over x), expert: 32 (over y, z, core).
Axes of the slice: x: 4, y: 4, z: 4, core: 2. Of those that a mesh axis runs over, the one named last changes fastest.
Arguments:
- section_input: bfloat16 [4, 4096, 2048], P('section', 'expert'), may hold values from -6 to 6
- fresh_batch: bfloat16 [4096, 2048], P('expert'), may hold values from -6 to 6
- attn_gain: float32 [4, 2048], P('section'), may hold values from 0.1 to 1.9
- query_gain: float32 [4, 64], P('section'), may hold values from 0.5 to 1.5
- key_gain: float32 [4, 64], P('section'), may hold values from 0.5 to 1.5
- kv_weight: bfloat16 [4, 2048, 512], P('section'), may hold values from -0.125 to 0.125
- out_weight: bfloat16 [4, 2048, 2048], P('section', 'expert'), may hold values from -0.125 to 0.125
- moe_gain: float32 [4, 2048], P('section'), may hold values from 0.1 to 1.9
- expert_gate_up: bfloat16 [4, 64, 2048, 1536], P('section', 'expert'), may hold values from -0.125 to 0.125
- expert_down: bfloat16 [4, 64, 768, 2048], P('section', 'expert'), may hold values from -0.21875 to 0.21875
- route_ids: int32 [4, 2, 4096, 8], P('section', None, 'expert'), may hold values from 0 to 63, all different within a row; in each aligned block of 128 rows (0 to 127, 128 to 255, ..., all dimensions but the last counted through in order) at most 18 rows name the same one
- route_weights: int32 [4, 2, 4096, 8], P('section', None, 'expert'), may hold values from 1 to 255
Outputs:
- layer_first: bfloat16 [4, 4096, 2048], P('section', 'expert')
- layer_second: bfloat16 [4, 4096, 2048], P('section', 'expert')
Inputs may be any that keep to these rules, and one draw needn't show every extreme that they name: `route_ids`: each row names 8 different experts. In the rows of one device (aligned blocks of 128 rows of one section and tick) no expert is named more than 18 times; one expert is named exactly 18 times in some or all blocks.
All inputs are finite; a program needn't handle non-finite values.
Results may differ from a plain program's by a relative error of at most 0.015.
Values may be sent and summed in bfloat16 or wider, within the bound.
A program may use at most 256 MiB of HBM per device.

v0:
```python
import jax
import jax.numpy as jnp
from jax import lax
from jax.sharding import PartitionSpec as P

HEAD = 64
QH = 32
KVH = 4
TOPK = 8


EPS = 1e-06


def shifted(x, axis, by):
    peers = lax.axis_size(axis)
    pairs = [(i, i + by) for i in range(peers) if 0 <= i + by < peers]
    return lax.ppermute(x, axis, pairs)


def rms_scale(values, gain):
    mean_sq = jnp.mean(values * values, axis=-1, keepdims=True)
    return values * lax.rsqrt(mean_sq + EPS) * gain


def slot_positions(ids, cap, experts_all):
    pairs = ids.shape[0] * ids.shape[1]
    flat = (ids.reshape(pairs, 1) == jnp.arange(experts_all, dtype=jnp.int32)[None, :]).astype(
        jnp.int32
    )
    rank = jnp.cumsum(flat, axis=0, dtype=jnp.int32) - flat
    slot = jnp.sum(rank * flat, axis=1, dtype=jnp.int32).reshape(ids.shape)
    return ids * cap + slot


def attend(attn_in, q_gain, k_gain, kv_w, place, seq_len):
    tok = attn_in.shape[0]
    kdim = KVH * HEAD
    group = QH // KVH
    kv_raw = jnp.dot(attn_in, kv_w, preferred_element_type=jnp.float32)
    keys = rms_scale(kv_raw[:, :kdim].reshape(tok, KVH, HEAD), k_gain).reshape(tok, kdim)
    keys_values = jnp.concatenate([keys, kv_raw[:, kdim:]], axis=1).astype(jnp.bfloat16)
    queries = (
        rms_scale(attn_in.astype(jnp.float32).reshape(tok, QH, HEAD), q_gain) * HEAD ** (-0.5)
    ).astype(jnp.bfloat16)
    queries = queries.reshape(tok, KVH, group, HEAD)
    first_row = place * tok
    qpos = first_row + jnp.arange(tok, dtype=jnp.int32)
    seq_first = first_row // seq_len * seq_len
    empty = (
        jnp.zeros((KVH, group, tok), jnp.float32),
        jnp.zeros((KVH, group, tok, HEAD), jnp.float32),
    )
    piece = lax.all_gather(keys_values, "expert", axis=0, tiled=True)
    start = jnp.int32(0)
    rows = piece.shape[0]

    def accumulate(state):
        kpos = jnp.arange(rows, dtype=jnp.int32)
        key_rows = piece[:, :kdim].reshape(rows, KVH, HEAD)
        value_rows = piece[:, kdim:].reshape(rows, KVH, HEAD)
        scores = jnp.einsum("tkgd,ukd->kgtu", queries, key_rows, preferred_element_type=jnp.float32)
        allowed = (kpos[None, :] <= qpos[:, None]) & (kpos[None, :] >= seq_first)
        expw = jnp.where(allowed, jnp.exp(scores), 0.0)
        mixed = jnp.einsum(
            "kgtu,ukd->kgtd",
            expw.astype(jnp.bfloat16),
            value_rows,
            preferred_element_type=jnp.float32,
        )
        return (jnp.sum(expw, axis=-1), mixed)

    needed = (start <= qpos[tok - 1]) & (start + rows > seq_first)
    total, mixed = lax.cond(needed, accumulate, lambda state: state, empty)
    out = mixed / total[..., None]
    return out.transpose(2, 0, 1, 3).reshape(tok, QH * HEAD).astype(jnp.bfloat16)


def experts_apply(rows, gate_up, down):
    local = gate_up.shape[0]
    width = down.shape[1]
    shaped = rows.reshape((rows.shape[0] // local, local) + rows.shape[1:])
    proj = jnp.einsum("nejd,edf->nejf", shaped, gate_up, preferred_element_type=jnp.float32)
    hidden = (jax.nn.silu(proj[..., :width]) * proj[..., width:]).astype(jnp.bfloat16)
    out = jnp.einsum("nejf,efd->nejd", hidden, down, preferred_element_type=jnp.float32).astype(
        jnp.bfloat16
    )
    return out.reshape(rows.shape)


def mixture(moe_in, ids, weight_ints, gate_up, down, cap, experts_all):
    tok, width = moe_in.shape
    topk = ids.shape[1]
    position = slot_positions(ids, cap, experts_all)
    token_of_pair = jnp.arange(tok * topk, dtype=jnp.int32) // topk
    source_rows = (
        jnp.full((experts_all * cap,), tok, jnp.int32).at[position.reshape(-1)].set(token_of_pair)
    )
    buffer = jnp.take(moe_in, source_rows, axis=0, mode="fill", fill_value=0).reshape(
        experts_all, cap, width
    )
    received = lax.all_to_all(buffer, "expert", split_axis=0, concat_axis=0, tiled=True)
    back = lax.all_to_all(
        experts_apply(received, gate_up, down), "expert", split_axis=0, concat_axis=0, tiled=True
    )
    picked = jnp.take(back.reshape(experts_all * cap, width), position, axis=0)
    gates = weight_ints.astype(jnp.float32) * (1.0 / 1024.0)
    return jnp.sum(picked.astype(jnp.float32) * gates[..., None], axis=1)


def body(
    section_input,
    fresh_batch,
    attn_gain,
    query_gain,
    key_gain,
    kv_weight,
    out_weight,
    moe_gain,
    expert_gate_up,
    expert_down,
    route_ids,
    route_weights,
):
    devices = lax.axis_size("expert")
    place = lax.axis_index("expert")
    tok = section_input.shape[1]
    experts_all = expert_gate_up.shape[1] * devices
    cap = tok * TOPK * 9 // (8 * experts_all)
    seq_len = tok * devices
    out_full = lax.all_gather(out_weight[0], "expert", axis=0, tiled=True)

    def layer(hidden, tick):
        h32 = hidden.astype(jnp.float32)
        attn_in = rms_scale(h32, attn_gain[0]).astype(jnp.bfloat16)
        attended = attend(attn_in, query_gain[0], key_gain[0], kv_weight[0], place, seq_len)
        after_attn = h32 + jnp.dot(attended, out_full, preferred_element_type=jnp.float32)
        moe_in = rms_scale(after_attn, moe_gain[0]).astype(jnp.bfloat16)
        moe = mixture(
            moe_in,
            route_ids[0, tick],
            route_weights[0, tick],
            expert_gate_up[0],
            expert_down[0],
            cap,
            experts_all,
        )
        return (after_attn + moe).astype(jnp.bfloat16)

    first_out = layer(section_input[0], 0)
    incoming = shifted(first_out, "section", 1)
    second_in = jnp.where(lax.axis_index("section") == 0, fresh_batch, incoming)
    second_out = layer(second_in, 1)
    return (first_out[None], second_out[None])


def solution(mesh):
    in_specs = (
        P("section", "expert", None),
        P("expert", None),
        P("section", None),
        P("section", None),
        P("section", None),
        P("section", None, None),
        P("section", "expert", None),
        P("section", None),
        P("section", "expert", None, None),
        P("section", "expert", None, None),
        P("section", None, "expert", None),
        P("section", None, "expert", None),
    )
    out_specs = (P("section", "expert", None), P("section", "expert", None))
    return jax.shard_map(body, mesh=mesh, in_specs=in_specs, out_specs=out_specs, check_vma=False)
```

profile of v0, /device:TPU:32, one launch (start us, length us, event | category | flops | bytes accessed | tf_op | source)
XLA Modules:
  0.0 755.2 jit_solution(11648395561190424141)
XLA Ops:
  7.2 1.4 fusion.63
  8.9 1.5 fusion.54
  12.3 0.7 all-gather.9.cloned.1.call-update
  13.1 1.2 copy.84
  15.1 0.7 eq.53
  18.3 0.7 fusion.75
  19.0 31.1 %reduce-window.14 = s32[64,8,128]{2,1,0:T(8,128)S(1)} reduce-window(s32[64,8,128]{2,1,0:T(8,128)} %fusion.75, s32[]{:T(128)} %constant.101.clone.1), window={size=1x1x128 pad=0_0x0_0x127_0}, to_apply=%region_7.8 | reduce-window | flops 8323072 | bytes 524292 | tf_op jit(solution)/shard_map/reduce-window
  50.2 0.8 slice.97
  51.0 1.1 copy.89
  52.2 0.8 copy.93
  53.0 0.7 mul.361
  53.8 0.8 fusion.74
  54.6 0.7 compare_select_fusion.1
  55.3 4.3 scatter_custom_fusion
  59.6 1.0 multiply_reduce_fusion.4
  60.7 1.9 multiply_convert_fusion.3
  62.5 67.2 %conditional.2 = (f32[4,8,128]{2,1,0:T(8,128)S(1)}, f32[4,8,128,64]{2,3,1,0:T(8,128)}) conditional(s32[]{:T(128)} %convert_element_type.164, () %tuple.26, (s32[128]{0:T(128)}, s32[]{:T(128)}, bf16[4096,512]{1,0:T(8,128)(2,1)}, bf16[128,4,8,64]{0,3,2,1:T(8,128)(2,1)}) %tuple.65), branch_computations={%region_3.4_spmd, %region_4.6_spmd} | conditional | flops 4363124736 | bytes 160459344 | solution.py:74
  62.5 6.5 copy.86
  69.0 4.8 fusion.88
  73.8 2.1 fusion.6
  76.0 26.9 %fusion.1 = (f32[4,8,128]{2,1,0:T(8,128)S(1)}, f32[4,4096,128,8]{2,1,3,0:T(8,128)}) fusion(pred[128,4096]{0,1:T(8,128)(4,1)S(1)} %fusion.6, bf16[4096,4,64,1]{0,2,3,1:T(8,128)(2,1)} %bitcast.212, bf16[128,4,8,64]{0,3,2,1:T(8,128)(2,1)S(1)} %copy-done.7), kind=kOutput, calls=%fused_computation.8 | convolution fusion | flops 2181033984 | bytes 70270976 | tf_op jit(solution)/shard_map/cond/branch_1_fun/tkgd,ukd->kgtu/dot_general | solution.py:62
  102.8 26.8 %fusion.2 = f32[4,8,128,64]{2,3,1,0:T(8,128)} fusion(bf16[4096,4,64,1]{0,2,3,1:T(8,128)(2,1)} %bitcast.214, f32[4,4096,128,8]{2,1,3,0:T(8,128)} %get-tuple-element.77, pred[128,4096]{0,1:T(8,128)(4,1)S(1)} %fusion.6), kind=kOutput, calls=%fused_computation.9 | convolution fusion | flops 2181038080 | bytes 70778880 | tf_op jit(solution)/shard_map/cond/branch_1_fun/kgtu,ukd->kgtd/dot_general | solution.py:65
  129.7 1.4 divide_convert_fusion.1
  131.1 4.7 multiply_reduce_fusion.3
  135.9 1.0 copy-done.2
  137.1 6.1 gather_fusion
  143.2 4.9 broadcast_select_fusion.1
  148.1 7.6 %reshape.336 = bf16[64,18,2048]{2,1,0:T(8,128)(2,1)} reshape(bf16[1152,2048]{1,0:T(8,128)(2,1)} %broadcast_select_fusion.1) | data formatting | bytes 9437184 | tf_op jit(solution)/shard_map/reshape | solution.py:99
  155.7 80.2 %all_to_all.20 = bf16[64,18,2048]{2,1,0:T(8,128)(2,1)S(1)} all-to-all(bf16[64,18,2048]{2,1,0:T(8,128)(2,1)} %reshape.336), channel_id=1, replica_groups=mesh['section'=4,'expert'=32] {'expert'}, dimensions={0} | all-to-all | bytes 9437184 | tf_op jit(solution)/shard_map/all_to_all | solution.py:102
  235.9 12.7 %fusion.30 = f32[32,2,18,1536]{3,0,2,1:T(8,128)} fusion(bf16[1,2,2048,1536]{3,2,1,0:T(8,128)(2,1)} %param.28, bf16[32,2,18,2048]{3,2,1,0:T(8,128)(2,1)S(1)} %bitcast.216), kind=kOutput, calls=%fused_computation.46 | convolution fusion | flops 7247757312 | bytes 24379392 | tf_op jit(solution)/shard_map/nejd,edf->nejf/dot_general | solution.py:83
  248.7 7.3 convert_bitcast_fusion.1
  256.0 5.4 copy.128
  261.4 6.1 all-to-all-start.1
  268.2 18.0 %reduce-window.16 = s32[64,8,128]{2,1,0:T(8,128)S(1)} reduce-window(s32[64,8,128]{2,1,0:T(8,128)S(1)} %fusion.76, s32[]{:T(128)} %constant.101.clone.1), window={size=1x1x128 pad=0_0x0_0x127_0}, to_apply=%region_19.22 | reduce-window | flops 8323072 | bytes 524292 | tf_op jit(solution)/shard_map/reduce-window.2
  287.5 67.1 %all-to-all-done.1 = bf16[64,18,2048]{2,1,0:T(8,128)(2,1)} async-done(((bf16[64,18,2048]{2,1,0:T(8,128)(2,1)}), bf16[64,18,2048]{2,1,0:T(8,128)(2,1)}, u32[]{:S(2)}, u32[]{:S(2)}) %all-to-all-start.1) | async-done | bytes 4718624 | tf_op jit(solution)/shard_map/all_to_all | solution.py:103
  354.6 7.8 %reshape.339 = bf16[1152,2048]{1,0:T(8,128)(2,1)} reshape(bf16[64,18,2048]{2,1,0:T(8,128)(2,1)} %all-to-all-done.1) | data formatting | bytes 9437184 | tf_op jit(solution)/shard_map/reshape | solution.py:106
  362.3 11.8 %gather_fusion.1 = bf16[1024,2048]{1,0:T(8,128)(2,1)} fusion(bf16[1152,2048]{1,0:T(8,128)(2,1)} %reshape.339, s32[1024]{0:T(1024)S(1)} %broadcast_clamp_fusion.1), kind=kCustom, calls=%fused_computation.1.clone | custom fusion | bytes 8392704 | tf_op jit(solution)/shard_map/jit(_take)/gather | solution.py:106
  374.1 5.7 multiply_reduce_fusion.1
  380.0 4.2 collective-permute-start
  384.2 10.2 %collective-permute-done = bf16[128,2048]{1,0:T(8,128)(2,1)} collective-permute-done((bf16[128,2048]{1,0:T(8,128)(2,1)S(1)}, bf16[128,2048]{1,0:T(8,128)(2,1)}, u32[]{:S(2)}, u32[]{:S(2)}) %collective-permute-start) | collective-permute-done | bytes 524320 | tf_op jit(solution)/shard_map/ppermute | solution.py:18
  396.4 4.3 scatter_custom_fusion.1
  401.0 1.3 copy.103
  402.6 1.3 bitcast_reduce_fusion
  404.2 37.5 %all-gather.7.cloned.1.call-done = bf16[4096,512]{1,0:T(8,128)(2,1)} async-done(((bf16[128,512]{1,0:T(8,128)(2,1)}), bf16[4096,512]{1,0:T(8,128)(2,1)}) %all-gather.7.cloned.1.call-update) | async-done | bytes 4194320 | tf_op jit(solution)/shard_map/all_gather | solution.py:54
  441.8 60.2 %conditional.3 = (f32[4,8,128]{2,1,0:T(8,128)S(1)}, f32[4,8,128,64]{2,3,1,0:T(8,128)S(1)}) conditional(s32[]{:T(128)} %convert_element_type.164, () %tuple.28, (s32[128]{0:T(128)S(1)}, s32[]{:T(128)}, bf16[4096,512]{1,0:T(8,128)(2,1)}, bf16[128,4,8,64]{0,3,2,1:T(8,128)(2,1)S(1)}) %tuple.66), branch_computations={%region_15.18_spmd, %region_16.20_spmd} | conditional | flops 4363124736 | bytes 158360080 | solution.py:74
  442.2 6.4 copy.104
  448.6 4.1 fusion.89
  452.7 2.1 fusion.14
  454.8 23.5 %fusion.9 = (f32[4,8,128]{2,1,0:T(8,128)S(1)}, f32[4,4096,128,8]{2,1,3,0:T(8,128)}) fusion(pred[128,4096]{0,1:T(8,128)(4,1)S(1)} %fusion.14, bf16[4096,4,64,1]{0,2,3,1:T(8,128)(2,1)S(1)} %bitcast.213, bf16[128,4,8,64]{0,3,2,1:T(8,128)(2,1)S(1)} %get-tuple-element.25), kind=kOutput, calls=%fused_computation.18 | convolution fusion | flops 2181033984 | bytes 70270976 | tf_op jit(solution)/shard_map/cond/branch_1_fun/tkgd,ukd->kgtu/dot_general | solution.py:62
  478.3 23.7 %fusion.10 = f32[4,8,128,64]{2,3,1,0:T(8,128)S(1)} fusion(bf16[4096,4,64,1]{0,2,3,1:T(8,128)(2,1)} %bitcast.215, f32[4,4096,128,8]{2,1,3,0:T(8,128)} %get-tuple-element.81, pred[128,4096]{0,1:T(8,128)(4,1)S(1)} %fusion.14), kind=kOutput, calls=%fused_computation.19 | convolution fusion | flops 2181038080 | bytes 70778880 | tf_op jit(solution)/shard_map/cond/branch_1_fun/kgtu,ukd->kgtd/dot_general | solution.py:65
  502.1 4.7 multiply_reduce_fusion.2
  507.0 6.1 gather_fusion.2
  513.1 4.9 broadcast_select_fusion
  518.1 7.6 %reshape.343 = bf16[64,18,2048]{2,1,0:T(8,128)(2,1)} reshape(bf16[1152,2048]{1,0:T(8,128)(2,1)} %broadcast_select_fusion) | data formatting | bytes 9437184 | tf_op jit(solution)/shard_map/reshape | solution.py:99
  525.6 78.1 %all_to_all.21 = bf16[64,18,2048]{2,1,0:T(8,128)(2,1)S(1)} all-to-all(bf16[64,18,2048]{2,1,0:T(8,128)(2,1)} %reshape.343), channel_id=1, replica_groups=mesh['section'=4,'expert'=32] {'expert'}, dimensions={0} | all-to-all | bytes 9437184 | tf_op jit(solution)/shard_map/all_to_all | solution.py:102
  603.7 12.7 %fusion.35 = f32[32,2,18,1536]{3,0,2,1:T(8,128)} fusion(bf16[1,2,2048,1536]{3,2,1,0:T(8,128)(2,1)} %param.28, bf16[32,2,18,2048]{3,2,1,0:T(8,128)(2,1)S(1)} %bitcast.217), kind=kOutput, calls=%fused_computation.47 | convolution fusion | flops 7247757312 | bytes 24379392 | tf_op jit(solution)/shard_map/nejd,edf->nejf/dot_general | solution.py:83
  616.4 7.3 convert_bitcast_fusion
  623.7 5.4 copy.131
  629.1 6.0 all-to-all-start.3
  635.6 86.6 %all-to-all-done.3 = bf16[64,18,2048]{2,1,0:T(8,128)(2,1)} async-done(((bf16[64,18,2048]{2,1,0:T(8,128)(2,1)}), bf16[64,18,2048]{2,1,0:T(8,128)(2,1)}, u32[]{:S(2)}, u32[]{:S(2)}) %all-to-all-start.3) | async-done | bytes 4718624 | tf_op jit(solution)/shard_map/all_to_all | solution.py:103
  722.2 7.8 %reshape.346 = bf16[1152,2048]{1,0:T(8,128)(2,1)} reshape(bf16[64,18,2048]{2,1,0:T(8,128)(2,1)} %all-to-all-done.3) | data formatting | bytes 9437184 | tf_op jit(solution)/shard_map/reshape | solution.py:106
  730.0 11.9 %gather_fusion.3 = bf16[1024,2048]{1,0:T(8,128)(2,1)} fusion(bf16[1152,2048]{1,0:T(8,128)(2,1)} %reshape.346, s32[1024]{0:T(1024)S(1)} %broadcast_clamp_fusion), kind=kCustom, calls=%fused_computation.3.clone | custom fusion | bytes 8392704 | tf_op jit(solution)/shard_map/jit(_take)/gather | solution.py:106
  741.9 5.6 multiply_reduce_fusion
  747.5 0.9 fusion.66
  (149 shorter events, 10.8 us)
Async XLA Ops:
  7.2 1.8 copy-start
  7.2 5.8 copy-start.10
  7.2 7.1 copy-start.12
  7.2 55.3 %all-gather.5.cloned.1.call-start = ((), (), s32[]{:S(2)}) async-start(), calls=%async_computation.4 | async-start | bytes 4325376 | tf_op jit(solution)/shard_map/all_gather | solution.py:54
  8.6 1.9 copy-start.18
  11.5 4.3 copy-start.15
  12.2 118.9 %all-gather.9.cloned.1.call-start = ((), (), s32[]{:S(2)}) async-start(), calls=%async_computation.6 | async-start | bytes 8650752 | tf_op jit(solution)/shard_map/all_gather | solution.py:131
  17.1 35.0 %copy-start.20 = (s32[128]{0:T(128)}, s32[128]{0:T(128)S(1)}, u32[]{:S(2)}) copy-start(s32[128]{0:T(128)S(1)} %iota_add_fusion) | copy-start | bytes 1540
  62.5 68.6 %copy-start.4 = (bf16[1,128,2048]{2,1,0:T(8,128)(2,1)S(1)}, bf16[1,128,2048]{2,1,0:T(8,128)(2,1)}, u32[]{:S(2)}) copy-start(bf16[1,128,2048]{2,1,0:T(8,128)(2,1)} %param.20) | copy-start | bytes 1572868
  69.0 4.8 copy-start.22
  69.0 6.9 copy-start.7
  131.1 5.8 copy-start.11
  135.9 1.1 copy-start.2
  155.7 93.0 %slice-start = ((s8[6291456]{0:T(1024)(128)(4,1)}), s8[4194304]{0:T(1024)(128)(4,1)S(1)}, s32[]{:S(2)}) async-start(s8[6291456]{0:T(1024)(128)(4,1)} %bitcast.241), calls=%async_computation.7 | async-start | bytes 8388608
  235.9 12.7 %slice-start.1 = ((s8[6291456]{0:T(1024)(128)(4,1)}), s8[2097152]{0:T(1024)(128)(4,1)S(1)}, s32[]{:S(2)}) async-start(s8[6291456]{0:T(1024)(128)(4,1)} %bitcast.241), calls=%async_computation.8 | async-start | bytes 4194304
  261.4 6.4 copy-start.14
  261.4 26.0 %copy-start.17 = (s32[1,2,128,8]{2,3,1,0:T(8,128)S(1)}, s32[1,2,128,8]{2,3,1,0:T(8,128)}, u32[]{:S(2)}) copy-start(s32[1,2,128,8]{2,3,1,0:T(8,128)} %param.31) | copy-start | bytes 24580
  261.4 93.2 %all-to-all-start.1 = ((bf16[64,18,2048]{2,1,0:T(8,128)(2,1)}), bf16[64,18,2048]{2,1,0:T(8,128)(2,1)}, u32[]{:S(2)}, u32[]{:S(2)}) async-start(bf16[64,18,2048]{2,1,0:T(8,128)(2,1)} %bitcast.208), calls=%async_computation.1 | async-start | bytes 12582912 | tf_op jit(solution)/shard_map/all_to_all | solution.py:103
  267.5 174.3 %all-gather.7.cloned.1.call-start = ((), (), s32[]{:S(2)}) async-start(), calls=%async_computation.5 | async-start | bytes 4325376 | tf_op jit(solution)/shard_map/all_gather | solution.py:54
  374.1 5.7 copy-start.3
  374.1 20.2 %copy-start.9 = (bf16[128,2048]{1,0:T(8,128)(2,1)S(1)}, bf16[128,2048]{1,0:T(8,128)(2,1)}, u32[]{:S(2)}) copy-start(bf16[128,2048]{1,0:T(8,128)(2,1)} %param.21) | copy-start | bytes 1572868
  379.8 15.6 %copy-start.16 = (f32[256]{0:T(256)S(1)}, f32[256]{0:T(256)}, u32[]{:S(2)}) copy-start(f32[256]{0:T(256)} %copy-done.15) | copy-start | bytes 3076
  379.9 16.3 %copy-start.13 = (s32[1,1,128,8]{2,3,1,0:T(8,128)S(1)}, s32[1,1,128,8]{2,3,1,0:T(8,128)}, u32[]{:S(2)}) copy-start(s32[1,1,128,8]{2,3,1,0:T(8,128)} %get-tuple-element.90) | copy-start | bytes 12292
  380.0 4.2 copy-start.8
  380.0 14.4 %collective-permute-start = (bf16[128,2048]{1,0:T(8,128)(2,1)S(1)}, bf16[128,2048]{1,0:T(8,128)(2,1)}, u32[]{:S(2)}, u32[]{:S(2)}) collective-permute-start(bf16[128,2048]{1,0:T(8,128)(2,1)S(1)} %add_convert_fusion.1), channel_id=1, source_target_pairs={{0,32},{32,64},{64,96},{1,33},{33,65},{65,97},{2,34},{34,66},{66,9... | collective-permute-start | bytes 1572872 | tf_op jit(solution)/shard_map/ppermute | solution.py:18
  394.6 7.7 %copy-start.5 = (bf16[128,2048]{1,0:T(8,128)(2,1)}, bf16[128,2048]{1,0:T(8,128)(2,1)S(1)}, u32[]{:S(2)}) copy-start(bf16[128,2048]{1,0:T(8,128)(2,1)S(1)} %get-tuple-element.71) | copy-start | bytes 1572868
  395.3 8.7 %copy-start.19 = (f32[1,64]{1,0:T(1,128)S(1)}, f32[1,64]{1,0:T(1,128)}, u32[]{:S(2)}) copy-start(f32[1,64]{1,0:T(1,128)} %param.23) | copy-start | bytes 772
  400.8 41.0 %copy-start.21 = (s32[128]{0:T(128)S(1)}, s32[128]{0:T(128)}, u32[]{:S(2)}) copy-start(s32[128]{0:T(128)} %copy-done.20) | copy-start | bytes 1540
  441.8 60.3 %copy-start.6 = (bf16[128,2048]{1,0:T(8,128)(2,1)S(1)}, bf16[128,2048]{1,0:T(8,128)(2,1)}, u32[]{:S(2)}) copy-start(bf16[128,2048]{1,0:T(8,128)(2,1)} %copy-done.5) | copy-start | bytes 1572868
  525.6 90.8 %slice-start.2 = ((s8[6291456]{0:T(1024)(128)(4,1)}), s8[4194304]{0:T(1024)(128)(4,1)S(1)}, s32[]{:S(2)}) async-start(s8[6291456]{0:T(1024)(128)(4,1)} %bitcast.243), calls=%async_computation.9 | async-start | bytes 8388608
  603.7 12.7 %slice-start.3 = ((s8[6291456]{0:T(1024)(128)(4,1)}), s8[2097152]{0:T(1024)(128)(4,1)S(1)}, s32[]{:S(2)}) async-start(s8[6291456]{0:T(1024)(128)(4,1)} %bitcast.243), calls=%async_computation.10 | async-start | bytes 4194304
  629.1 93.1 %all-to-all-start.3 = ((bf16[64,18,2048]{2,1,0:T(8,128)(2,1)}), bf16[64,18,2048]{2,1,0:T(8,128)(2,1)}, u32[]{:S(2)}, u32[]{:S(2)}) async-start(bf16[64,18,2048]{2,1,0:T(8,128)(2,1)} %bitcast.209), calls=%async_computation.3 | async-start | bytes 12582912 | tf_op jit(solution)/shard_map/all_to_all | solution.py:103
  730.0 18.5 %copy-start.1 = (bf16[1,2048,512]{2,1,0:T(8,128)(2,1)S(1)}, bf16[1,2048,512]{2,1,0:T(8,128)(2,1)}, u32[]{:S(2)}) copy-start(bf16[1,2048,512]{2,1,0:T(8,128)(2,1)} %param.25) | copy-start | bytes 6291460
Sparse Core Ops, SparseCore 0:
  12.3 48.1 all-gather.4
  62.8 52.3 all-gather.8
  396.3 45.4 all-gather.6
where the time goes:
time: 767 us; the launch traced here: 755 us
  waiting for transfers between devices  202 us (26%)
  blocking collectives  158 us (21%)
  matrix products  152 us (20%)
  local copies, waits for them, and re-layouts  121 us (16%)
  other arithmetic  89.2 us (12%)
  starting transfers between devices  16.6 us (2%)
  between operations  15.3 us (2%)
    all_to_all x2, blocking collectives, mixture(): lax.all_to_all(buffer, 'expert', split_axis=0, concat_axis=0, tiled=True)  158 us
    all_to_all x2, waiting for transfers between devices, mixture(): lax.all_to_all(experts_apply(received, gate_up, down), 'expert', split_ax...  154 us
    dot_general x2, matrix products, accumulate(): jnp.einsum('kgtu,ukd->kgtd', expw.astype(jnp.bfloat16), value_rows, prefe...  50.4 us
    dot_general x2, matrix products, accumulate(): jnp.einsum('tkgd,ukd->kgtu', queries, key_rows, preferred_element_type=jn...  50.3 us
    another operation x8, other arithmetic  49.5 us
    all_gather x2, waiting for transfers between devices, attend(): piece = lax.all_gather(keys_values, 'expert', axis=0, tiled=True)  37.6 us
    dot_general x2, matrix products, experts_apply(): jnp.einsum('nejd,edf->nejf', shaped, gate_up, preferred_element_type=jnp....  25.5 us
    gather x2, local copies, waits for them, and re-layouts, mixture(): picked = jnp.take(back.reshape(experts_all * cap, width), position, axis=0)  23.7 us
  transfers between devices with their start and end apart: 6, of which 4 were waited for; matrix products, arithmetic and copies ran while one was open for 19% of the time, Pallas kernels for 0%

commit v1 on v0

--- a/solution.py
+++ b/solution.py
@@ -1,6 +1,9 @@
+import functools
 import jax
 import jax.numpy as jnp
 from jax import lax
+from jax.experimental import pallas as pl
+from jax.experimental.pallas import tpu as pltpu
 from jax.sharding import PartitionSpec as P
 
 HEAD = 64
@@ -21,16 +24,6 @@
 def rms_scale(values, gain):
     mean_sq = jnp.mean(values * values, axis=-1, keepdims=True)
     return values * lax.rsqrt(mean_sq + EPS) * gain
-
-
-def slot_positions(ids, cap, experts_all):
-    pairs = ids.shape[0] * ids.shape[1]
-    flat = (ids.reshape(pairs, 1) == jnp.arange(experts_all, dtype=jnp.int32)[None, :]).astype(
-        jnp.int32
-    )
-    rank = jnp.cumsum(flat, axis=0, dtype=jnp.int32) - flat
-    slot = jnp.sum(rank * flat, axis=1, dtype=jnp.int32).reshape(ids.shape)
-    return ids * cap + slot
 
 
 def attend(attn_in, q_gain, k_gain, kv_w, place, seq_len):
@@ -76,36 +69,377 @@
     return out.transpose(2, 0, 1, 3).reshape(tok, QH * HEAD).astype(jnp.bfloat16)
 
 
-def experts_apply(rows, gate_up, down):
-    local = gate_up.shape[0]
-    width = down.shape[1]
-    shaped = rows.reshape((rows.shape[0] // local, local) + rows.shape[1:])
-    proj = jnp.einsum("nejd,edf->nejf", shaped, gate_up, preferred_element_type=jnp.float32)
-    hidden = (jax.nn.silu(proj[..., :width]) * proj[..., width:]).astype(jnp.bfloat16)
-    out = jnp.einsum("nejf,efd->nejd", hidden, down, preferred_element_type=jnp.float32).astype(
-        jnp.bfloat16
+MESH = pl.DeviceIdType.MESH
+CHUNKS = 4
+BF16 = jnp.bfloat16
+F32 = jnp.float32
+
+
+def route_info(ids, weight_ints, experts_all):
+    chosen = ids[:, :, None] == jnp.arange(experts_all, dtype=jnp.int32)[None, None, :]
+    member = jnp.any(chosen, axis=1)
+    gates = weight_ints.astype(F32) * (1.0 / 1024.0)
+    weight = jnp.sum(jnp.where(chosen, gates[..., None], 0.0), axis=1)
+    tok = ids.shape[0]
+    before = jnp.tril(jnp.ones((tok, tok), BF16), -1)
+    rank = jnp.dot(before, member.astype(BF16), preferred_element_type=F32)
+    return jnp.concatenate([jnp.where(member, rank, -1.0).T, weight.T], axis=0)
+
+
+def moe_kernel(
+    cap,
+    x_ref,
+    after_ref,
+    info_ref,
+    gu_hbm,
+    dn_hbm,
+    out_ref,
+    xg,
+    sb,
+    xb,
+    bb,
+    pb,
+    pr,
+    pf,
+    tot,
+    infog,
+    sel,
+    cw,
+    ct,
+    gu,
+    dn,
+    acc,
+    hid,
+    si,
+    ri,
+    s1,
+    r1,
+    s2,
+    r2,
+    s3,
+    r3,
+    s4,
+    r4,
+    wsem,
+):
+    me = lax.axis_index("expert")
+    sec = lax.axis_index("section")
+    y, z, c = me // 8, (me // 2) % 4, me % 2
+    g = c * z + (1 - c) * y
+    ln = c * y + (1 - c) * z
+    chunks, width = xg.shape[0], xg.shape[3]
+    rows = 2 * 4 * cap
+    half = 4 * cap
+    my_slot = 4 * c + ln
+    my_line = 2 * ln + c
+
+    def relay(gp):
+        return 2 * (c * (4 * ln + gp) + (1 - c) * (4 * gp + ln)) + c
+
+    def line_dev(i):
+        return 2 * (c * (4 * (i // 2) + g) + (1 - c) * (4 * g + i // 2)) + i % 2
+
+    def slot_dev(s):
+        t, l0 = s // 4, s % 4
+        return (1 - t) * (8 * y + 2 * l0) + t * (8 * l0 + 2 * z + 1)
+
+    def slot_line(s):
+        t = s // 4
+        return 2 * ((1 - t) * z + t * y) + c
+
+    def remote(src, dst, send, recv, dev):
+        return pltpu.make_async_remote_copy(
+            src_ref=src,
+            dst_ref=dst,
+            send_sem=send,
+            recv_sem=recv,
+            device_id=(sec, dev),
+            device_id_type=MESH,
+        )
+
+    def info_copy(k):
+        gp = (g + k) % 4
+        return remote(infog.at[g], infog.at[g], si.at[k], ri.at[g], relay(gp))
+
+    def info_arrival(k):
+        gp = (g + k) % 4
+        return remote(infog.at[gp], infog.at[gp], si.at[k], ri.at[gp], relay(gp))
+
+    def gather_copy(j, k):
+        gp = (g + k) % 4
+        return remote(xg.at[j, g], xg.at[j, g], s1.at[j, k], r1.at[j, g], relay(gp))
+
+    def gather_arrival(j, k):
+        gp = (g + k) % 4
+        return remote(xg.at[j, gp], xg.at[j, gp], s1.at[j, k], r1.at[j, gp], relay(gp))
+
+    def out_copy(j, i):
+        return remote(sb.at[j, i], xb.at[j, my_slot], s2.at[j, i], r2.at[j, my_slot], line_dev(i))
+
+    def out_arrival(j, s):
+        return remote(xb.at[j, s], xb.at[j, s], s2.at[j, s], r2.at[j, s], slot_dev(s))
+
+    def back_copy(j, s):
+        i = slot_line(s)
+        return remote(xb.at[j, s], bb.at[j, i], s3.at[j, s], r3.at[j, i], slot_dev(s))
+
+    def back_arrival(j, i):
+        return remote(bb.at[j, i], bb.at[j, i], s3.at[j, i], r3.at[j, i], line_dev(i))
+
+    def sum_copy(j, k):
+        gp = (g + k) % 4
+        return remote(pb.at[j, gp], pr.at[j, g], s4.at[j, k], r4.at[j, g], relay(gp))
+
+    def sum_arrival(j, k):
+        gp = (g + k) % 4
+        return remote(pr.at[j, gp], pr.at[j, gp], s4.at[j, k], r4.at[j, gp], relay(gp))
+
+    def each(n, first=0):
+        def wrap(f):
+            def step(i, carry):
+                f(i)
+                return carry
+
+            lax.fori_loop(first, n, step, 0)
+
+        return wrap
+
+    gu_copy = pltpu.make_async_copy(gu_hbm, gu, wsem.at[0])
+    dn_copy = pltpu.make_async_copy(dn_hbm, dn, wsem.at[1])
+
+    barrier = pltpu.get_barrier_semaphore()
+
+    def greet(dev):
+        pl.semaphore_signal(barrier, inc=1, device_id=(sec, dev), device_id_type=MESH)
+
+    @each(8, 1)
+    def _(k):
+        greet(8 * y + (2 * z + c + k) % 8)
+
+    @each(4, 1)
+    def _(k):
+        greet(8 * ((y + k) % 4) + 2 * z)
+        greet(8 * ((y + k) % 4) + 2 * z + 1)
+
+    infog[g] = info_ref[...]
+    for j in range(chunks):
+        xg[j, g] = x_ref[:, j * width : (j + 1) * width]
+    pl.semaphore_wait(barrier, 13)
+
+    @each(4, 1)
+    def _(k):
+        info_copy(k).start()
+
+    @each(chunks)
+    def _(j):
+        @each(4, 1)
+        def _(k):
+            gather_copy(j, k).start()
+
+    gu_copy.start()
+    dn_copy.start()
+    acc[...] = jnp.zeros_like(acc)
+
+    row = lax.broadcasted_iota(jnp.int32, (half, 512), 0)
+    lane = lax.broadcasted_iota(jnp.int32, (half, 512), 1)
+    block_of_row = (
+        (row >= cap).astype(jnp.int32)
+        + (row >= 2 * cap).astype(jnp.int32)
+        + (row >= 3 * cap).astype(jnp.int32)
     )
-    return out.reshape(rows.shape)
-
-
-def mixture(moe_in, ids, weight_ints, gate_up, down, cap, experts_all):
-    tok, width = moe_in.shape
-    topk = ids.shape[1]
-    position = slot_positions(ids, cap, experts_all)
-    token_of_pair = jnp.arange(tok * topk, dtype=jnp.int32) // topk
-    source_rows = (
-        jnp.full((experts_all * cap,), tok, jnp.int32).at[position.reshape(-1)].set(token_of_pair)
-    )
-    buffer = jnp.take(moe_in, source_rows, axis=0, mode="fill", fill_value=0).reshape(
-        experts_all, cap, width
-    )
-    received = lax.all_to_all(buffer, "expert", split_axis=0, concat_axis=0, tiled=True)
-    back = lax.all_to_all(
-        experts_apply(received, gate_up, down), "expert", split_axis=0, concat_axis=0, tiled=True
-    )
-    picked = jnp.take(back.reshape(experts_all * cap, width), position, axis=0)
-    gates = weight_ints.astype(jnp.float32) * (1.0 / 1024.0)
-    return jnp.sum(picked.astype(jnp.float32) * gates[..., None], axis=1)
+    pattern = jnp.where(block_of_row == lane // 128, row - cap * block_of_row, -5).astype(F32)
+
+    @each(4, 1)
+    def _(k):
+        info_arrival(k).wait_recv()
+
+    @each(8)
+    def _(i):
+        dev = line_dev(i)
+        picks, gates = [], []
+        for e in range(2):
+            at = 2 * dev + e
+            rank = jnp.concatenate([infog[b, pl.ds(at, 1), :] for b in range(4)], axis=1)
+            gate = jnp.concatenate([infog[b, pl.ds(64 + at, 1), :] for b in range(4)], axis=1)
+            hit = rank == pattern
+            picks.append(jnp.where(hit, 1.0, 0.0))
+            gates.append(jnp.where(hit, gate, 0.0))
+        at = pl.multiple_of(i * rows, 16)
+        sel[pl.ds(at, rows), :] = jnp.concatenate(picks, axis=0).astype(BF16)
+        cw[pl.ds(at, rows), :] = jnp.concatenate(gates, axis=0).astype(BF16)
+
+    @each(chunks)
+    def _(j):
+        @each(4, 1)
+        def _(k):
+            gather_arrival(j, k).wait_recv()
+
+        @each(width // 256)
+        def _(n):
+            cols = pl.ds(pl.multiple_of(n * 256, 256), 256)
+            held = xg[j, :, :, cols].reshape(512, 256)
+            got = jnp.dot(sel[...], held, preferred_element_type=F32)
+            sb[j, :, :, cols] = got.astype(BF16).reshape(8, rows, 256)
+
+        @each(8, 1)
+        def _(k):
+            out_copy(j, (my_line + k) % 8).start()
+
+        xb[j, my_slot] = sb[j, my_line]
+
+    for m in range(8 * rows // 128):
+        ct[:, m * 128 : (m + 1) * 128] = (
+            cw[m * 128 : (m + 1) * 128, :].astype(F32).T.astype(BF16)
+        )
+
+    gu_copy.wait()
+
+    @each(chunks)
+    def _(j):
+        @each(8, 1)
+        def _(k):
+            out_arrival(j, (my_slot + k) % 8).wait_recv()
+
+        for e in range(2):
+            first = e * (rows - 80)
+
+            @each(acc.shape[2] // 256)
+            def _(n):
+                cols = pl.ds(pl.multiple_of(n * 256, 256), 256)
+                lhs = xb[j, :, first : first + 80, :].reshape(640, width)
+                rhs = gu[e, pl.ds(pl.multiple_of(j * width, width), width), cols]
+                acc[e, :, cols] += jnp.dot(lhs, rhs, preferred_element_type=F32)
+
+    ff = hid.shape[2]
+    for e in range(2):
+
+        @each(640 // 128)
+        def _(m):
+            at = pl.ds(pl.multiple_of(m * 128, 128), 128)
+            hid[e, at, :] = (jax.nn.silu(acc[e, at, :ff]) * acc[e, at, ff:]).astype(BF16)
+
+    dn_copy.wait()
+
+    @each(chunks)
+    def _(j):
+        @each(width // 256)
+        def _(n):
+            cols = pl.ds(pl.multiple_of(n * 256, 256), 256)
+            at = pl.ds(pl.multiple_of(j * width + n * 256, 256), 256)
+            made = [
+                jnp.dot(hid[e], dn[e, :, at], preferred_element_type=F32).reshape(8, 80, 256)
+                for e in range(2)
+            ]
+            line = lax.broadcasted_iota(jnp.int32, (8, 16, 256), 1)
+            shared = jnp.where(line < 8, made[0][:, 64:80], made[1][:, 0:16])
+            xb[j, :, 0:64, cols] = made[0][:, 0:64].astype(BF16)
+            xb[j, :, 64:80, cols] = shared.astype(BF16)
+            xb[j, :, 80:144, cols] = made[1][:, 16:80].astype(BF16)
+
+        @each(8, 1)
+        def _(k):
+            back_copy(j, (my_slot + k) % 8).start()
+
+        bb[j, my_line] = xb[j, my_slot]
+
+    @each(chunks)
+    def _(j):
+        @each(8, 1)
+        def _(k):
+            back_arrival(j, (my_line + k) % 8).wait_recv()
+
+        @each(width // 256)
+        def _(n):
+            cols = pl.ds(pl.multiple_of(n * 256, 256), 256)
+            at = pl.ds(pl.multiple_of(j * width + n * 256, 256), 256)
+            part = jnp.dot(
+                ct[...], bb[j, :, :, cols].reshape(8 * rows, 256), preferred_element_type=F32
+            ).reshape(4, 128, 256)
+            pf[...] = part
+            pb[j, :, :, cols] = part.astype(BF16)
+            tot[:, at] = after_ref[:, at] + pf[g]
+
+        @each(4, 1)
+        def _(k):
+            sum_copy(j, k).start()
+
+    @each(chunks)
+    def _(j):
+        at = pl.ds(pl.multiple_of(j * width, width), width)
+
+        @each(4, 1)
+        def _(k):
+            sum_arrival(j, k).wait_recv()
+            tot[:, at] += pr[j, (g + k) % 4].astype(F32)
+
+        out_ref[:, at] = tot[:, at].astype(BF16)
+
+    @each(4, 1)
+    def _(k):
+        info_copy(k).wait_send()
+
+    @each(chunks)
+    def _(j):
+        @each(4, 1)
+        def _(k):
+            gather_copy(j, k).wait_send()
+            sum_copy(j, k).wait_send()
+
+        @each(8, 1)
+        def _(k):
+            out_copy(j, (my_line + k) % 8).wait_send()
+            back_copy(j, (my_slot + k) % 8).wait_send()
+
+
+def moe_layer(moe_in, after_attn, info, gate_up, down, cap, tick):
+    tok, d = moe_in.shape
+    ff = down.shape[1]
+    w = d // CHUNKS
+    rows = 8 * cap
+    vmem = pl.BlockSpec(memory_space=pltpu.VMEM)
+    hbm = pl.BlockSpec(memory_space=pl.ANY)
+    dma = pltpu.SemaphoreType.DMA
+    return pl.pallas_call(
+        functools.partial(moe_kernel, cap),
+        out_shape=jax.ShapeDtypeStruct((tok, d), BF16),
+        in_specs=[vmem, vmem, vmem, hbm, hbm],
+        out_specs=vmem,
+        scratch_shapes=[
+            pltpu.VMEM((CHUNKS, 4, tok, w), BF16),
+            pltpu.VMEM((CHUNKS, 8, rows, w), BF16),
+            pltpu.VMEM((CHUNKS, 8, rows, w), BF16),
+            pltpu.VMEM((CHUNKS, 8, rows, w), BF16),
+            pltpu.VMEM((CHUNKS, 4, tok, w), BF16),
+            pltpu.VMEM((CHUNKS, 4, tok, w), BF16),
+            pltpu.VMEM((4, tok, 256), F32),
+            pltpu.VMEM((tok, d), F32),
+            pltpu.VMEM((4, 128, tok), F32),
+            pltpu.VMEM((8 * rows, 4 * tok), BF16),
+            pltpu.VMEM((8 * rows, 4 * tok), BF16),
+            pltpu.VMEM((4 * tok, 8 * rows), BF16),
+            pltpu.VMEM(gate_up.shape, BF16),
+            pltpu.VMEM(down.shape, BF16),
+            pltpu.VMEM((2, 640, 2 * ff), F32),
+            pltpu.VMEM((2, 640, ff), BF16),
+            dma((4,)),
+            dma((4,)),
+            dma((CHUNKS, 4)),
+            dma((CHUNKS, 4)),
+            dma((CHUNKS, 8)),
+            dma((CHUNKS, 8)),
+            dma((CHUNKS, 8)),
+            dma((CHUNKS, 8)),
+            dma((CHUNKS, 4)),
+            dma((CHUNKS, 4)),
+            dma((2,)),
+        ],
+        compiler_params=pltpu.CompilerParams(
+            collective_id=4 + tick, has_side_effects=True, vmem_limit_bytes=64 << 20
+        ),
+        cost_estimate=pl.CostEstimate(
+            flops=12 * 10**9, bytes_accessed=20 * 10**6, transcendentals=10**6
+        ),
+    )(moe_in, after_attn, info, gate_up, down)
 
 
 def body(
@@ -128,6 +462,7 @@
     experts_all = expert_gate_up.shape[1] * devices
     cap = tok * TOPK * 9 // (8 * experts_all)
     seq_len = tok * devices
+    infos = [route_info(route_ids[0, t], route_weights[0, t], experts_all) for t in range(2)]
     out_full = lax.all_gather(out_weight[0], "expert", axis=0, tiled=True)
 
     def layer(hidden, tick):
@@ -136,16 +471,9 @@
         attended = attend(attn_in, query_gain[0], key_gain[0], kv_weight[0], place, seq_len)
         after_attn = h32 + jnp.dot(attended, out_full, preferred_element_type=jnp.float32)
         moe_in = rms_scale(after_attn, moe_gain[0]).astype(jnp.bfloat16)
-        moe = mixture(
-            moe_in,
-            route_ids[0, tick],
-            route_weights[0, tick],
-            expert_gate_up[0],
-            expert_down[0],
-            cap,
-            experts_all,
+        return moe_layer(
+            moe_in, after_attn, infos[tick], expert_gate_up[0], expert_down[0], cap, tick
         )
-        return (after_attn + moe).astype(jnp.bfloat16)
 
     first_out = layer(section_input[0], 0)
     incoming = shifted(first_out, "section", 1)

time: 767 us -> 468 us (0.61); the launches traced: 755 us -> 465 us
  Pallas kernels: 0 us -> 186 us
  blocking collectives: 158 us -> 0 us
  waiting for transfers between devices: 202 us -> 90.5 us
  local copies, waits for them, and re-layouts: 121 us -> 32 us
  other arithmetic: 89.2 us -> 22.7 us
  matrix products: 152 us -> 115 us
  starting transfers between devices: 16.6 us -> 3.55 us
    pallas_call x0 -> x2, Pallas kernels: none -> 186 us  [moe_layer(): pl.pallas_call(functools.partial(moe_kernel, cap), out_shape=jax.ShapeDty...]
    all_to_all x2 -> x0, blocking collectives: 158 us -> none  [mixture(): lax.all_to_all(buffer, 'expert', split_axis=0, concat_axis=0, tiled=True)]
    all_to_all x2 -> x0, waiting for transfers between devices: 154 us -> none  [mixture(): lax.all_to_all(experts_apply(received, gate_up, down), 'expert', split_ax...]
    another operation x8 -> x2, other arithmetic: 49.5 us -> 0.72 us
    reshape x10 -> x0, local copies, waits for them, and re-layouts: 41.7 us -> none  [the longest x2 15.5 us: mixture(): picked = jnp.take(back.reshape(experts_all * cap, width), position, axis=0)]
    all_gather x2, waiting for transfers between devices: 37.6 us -> 79.2 us  [attend(): piece = lax.all_gather(keys_values, 'expert', axis=0, tiled=True)]
    dot_general x4 -> x2, matrix products: 40.1 us -> 0.4 us  [route_info(): rank = jnp.dot(before, member.astype(BF16), preferred_element_type=F32)]
    gather x4 -> x0, local copies, waits for them, and re-layouts: 35.8 us -> none  [the longest x2 23.7 us: mixture(): picked = jnp.take(back.reshape(experts_all * cap, width), position, axis=0)]
  transfers between devices with their start and end apart: 6 -> 4, of which waited for: 4 -> 3; matrix products, arithmetic and copies ran while one was open for 19% -> 17% of each run, Pallas kernels for 0% -> 0%
where the time goes in v1:
time: 468 us; the launch traced here: 465 us
  Pallas kernels  186 us (40%)
  matrix products  115 us (25%)
  waiting for transfers between devices  90.5 us (19%)
  local copies, waits for them, and re-layouts  32 us (7%)
  other arithmetic  22.7 us (5%)
  between operations  14.9 us (3%)
    pallas_call x2, Pallas kernels, moe_layer(): pl.pallas_call(functools.partial(moe_kernel, cap), out_shape=jax.ShapeDty...  186 us
    all_gather x2, waiting for transfers between devices, attend(): piece = lax.all_gather(keys_values, 'expert', axis=0, tiled=True)  79.2 us
    dot_general x2, matrix products, accumulate(): jnp.einsum('kgtu,ukd->kgtd', expw.astype(jnp.bfloat16), value_rows, prefe...  51.4 us
    dot_general x2, matrix products, accumulate(): jnp.einsum('tkgd,ukd->kgtu', queries, key_rows, preferred_element_type=jn...  48.9 us
    another operation x2, local copies, waits for them, and re-layouts  12.9 us
    ppermute x1, waiting for transfers between devices, shifted(): return lax.ppermute(x, axis, pairs)  10.6 us
    dot_general x2, matrix products, layer(): jnp.dot(attended, out_full, preferred_element_type=jnp.float32)  9.55 us
  transfers between devices with their start and end apart: 4, of which 3 were waited for; matrix products, arithmetic and copies ran while one was open for 17% of the time, Pallas kernels for 0%

profile of v1, /device:TPU:32, one launch (start us, length us, event | category | flops | bytes accessed | tf_op | source)
XLA Modules:
  0.0 464.8 jit_solution(7630811919858672092)
XLA Ops:
  7.2 0.0 all-gather.5.cloned.1.call-start
  7.3 1.2 fusion.33
  8.5 2.3 fusion.28
  10.8 0.1 copy.42
  11.0 0.1 copy.43
  11.1 0.7 mul.264
  11.7 0.1 mul.265
  11.8 0.7 pad_maximum_fusion
  12.5 0.0 all-gather.9.cloned.1.call-start
  12.6 0.7 all-gather.9.cloned.1.call-update
  13.3 0.8 mul.275
  14.1 1.2 copy.44
  15.4 0.5 broadcast.245
  15.9 0.7 reduce.5
  16.6 0.1 mul.270
  16.6 0.5 iota_add_fusion.1
  17.2 1.2 slice.42
  19.0 0.7 fusion.38
  19.7 0.7 select_reduce_fusion
  20.4 0.2 convolution_select_fusion.1
  20.6 0.6 pad_maximum_fusion.2.info_ref
  21.2 0.4 multiply_reduce_fusion.2
  21.6 1.2 multiply_convert_fusion.3
  22.8 38.0 %all-gather.5.cloned.1.call-done = bf16[4096,512]{1,0:T(8,128)(2,1)} async-done(((bf16[128,512]{1,0:T(8,128)(2,1)}), bf16[4096,512]{1,0:T(8,128)(2,1)}) %all-gather.5.cloned.1.call-update) | async-done | bytes 4194320 | tf_op jit(solution)/shard_map/all_gather | solution.py:47
  60.8 65.0 %conditional.2 = (f32[4,8,128]{2,1,0:T(8,128)S(1)}, f32[4,8,128,64]{2,3,1,0:T(8,128)}) conditional(s32[]{:T(128)} %convert_element_type.122, () %tuple.24, (s32[128]{0:T(128)}, s32[]{:T(128)}, bf16[4096,512]{1,0:T(8,128)(2,1)}, bf16[128,4,8,64]{0,3,2,1:T(8,128)(2,1)}) %tuple.25), branch_computations={%region_3.4_spmd, %region_4.6_spmd} | conditional | flops 4363124736 | bytes 160457264 | solution.py:67
  60.8 6.5 %copy.46 = bf16[4096,512]{0,1:T(8,128)(2,1)} copy(bf16[4096,512]{1,0:T(8,128)(2,1)} %get-tuple-element.52) | data formatting | bytes 8388608 | tf_op jit(solution)/shard_map
  67.2 4.1 fusion.55
  71.3 2.7 fusion.6
  74.1 24.4 %fusion.1 = (f32[4,8,128]{2,1,0:T(8,128)S(1)}, f32[4,4096,128,8]{2,1,3,0:T(8,128)}) fusion(pred[128,4096]{0,1:T(8,128)(4,1)S(1)} %fusion.6, bf16[4096,4,64,1]{0,2,3,1:T(8,128)(2,1)S(1)} %bitcast.117, bf16[128,4,8,64]{0,3,2,1:T(8,128)(2,1)S(1)} %copy-done.4), kind=kOutput, calls=%fused_computation.2 | convolution fusion | flops 2181033984 | bytes 70270976 | tf_op jit(solution)/shard_map/cond/branch_1_fun/tkgd,ukd->kgtu/dot_general | solution.py:55
  98.5 27.3 %fusion.2 = f32[4,8,128,64]{2,3,1,0:T(8,128)} fusion(bf16[4096,4,64,1]{0,2,3,1:T(8,128)(2,1)} %bitcast.119, f32[4,4096,128,8]{2,1,3,0:T(8,128)} %get-tuple-element.63, pred[128,4096]{0,1:T(8,128)(4,1)S(1)} %fusion.6), kind=kOutput, calls=%fused_computation.3 | convolution fusion | flops 2181038080 | bytes 70778880 | tf_op jit(solution)/shard_map/cond/branch_1_fun/kgtu,ukd->kgtd/dot_general | solution.py:58
  125.8 1.3 divide_convert_fusion.1
  127.2 4.7 %multiply_reduce_fusion.1 = (f32[128]{0:T(128)S(1)}, f32[128,2048]{1,0:T(8,128)S(1)}) fusion(bf16[128,2048]{0,1:T(8,128)(2,1)S(1)} %bitcast.122, bf16[1,2048,2048]{2,1,0:T(8,128)(2,1)} %all-gather.9.cloned.1.call-done, bf16[1,128,2048]{2,1,0:T(8,128)(2,1)S(1)} %copy-done), kind=kOutput, calls=%fused_computation.45 | convolution fusion | flops 1074790272 | bytes 10486272 | tf_op jit(solution)/shard_map/dot_general | solution.py:472
  131.9 1.0 copy-done.3
  132.9 0.9 multiply_convert_fusion.2.x_ref
  133.9 93.1 %shard_map.131 = bf16[128,2048]{1,0:T(8,128)(2,1)} custom-call(bf16[128,2048]{1,0:T(8,128)(2,1)} %multiply_convert_fusion.2.x_ref, f32[128,2048]{1,0:T(8,128)} %copy-done.3, f32[128,128]{1,0:T(8,128)} %pad_maximum_fusion.2.info_ref, bf16[2,2048,1536]{2,1,0:T(8,128)(2,1)} %bitcast.139, bf16[2,768,2048]{2,1,0:T(8,128)(2,1)} %bitcast.141), custom_call_target="tpu_custom_call" | custom-call | flops 12000000000 | bytes 20000000 | tf_op jit(solution)/shard_map/pallas_call | solution.py:402
  227.0 3.4 collective-permute-start
  230.4 10.6 %collective-permute-done = bf16[128,2048]{1,0:T(8,128)(2,1)S(1)} collective-permute-done((bf16[128,2048]{1,0:T(8,128)(2,1)}, bf16[128,2048]{1,0:T(8,128)(2,1)S(1)}, u32[]{:S(2)}, u32[]{:S(2)}) %collective-permute-start) | collective-permute-done | bytes 524320 | tf_op jit(solution)/shard_map/ppermute | solution.py:21
  241.0 1.3 fusion.30
  242.3 2.3 fusion.26
  244.7 0.1 copy.47
  244.8 0.1 copy.48
  244.9 0.7 multiply_convert_fusion.7
  245.6 0.7 pad_maximum_fusion.1
  246.3 0.2 convolution_select_fusion
  246.5 0.6 pad_maximum_fusion.3.info_ref
  247.2 0.2 convert_multiply_fusion.2
  247.4 1.3 copy.50
  248.7 0.3 copy.49
  249.1 1.3 bitcast_reduce_fusion
  250.4 1.0 multiply_convert_fusion.1
  251.4 41.2 %all-gather.7.cloned.1.call-done = bf16[4096,512]{1,0:T(8,128)(2,1)} async-done(((bf16[128,512]{1,0:T(8,128)(2,1)}), bf16[4096,512]{1,0:T(8,128)(2,1)}) %all-gather.7.cloned.1.call-update) | async-done | bytes 4194320 | tf_op jit(solution)/shard_map/all_gather | solution.py:47
  292.7 60.5 %conditional.3 = (f32[4,8,128]{2,1,0:T(8,128)S(1)}, f32[4,8,128,64]{2,3,1,0:T(8,128)}) conditional(s32[]{:T(128)} %convert_element_type.122, () %tuple.26, (s32[128]{0:T(128)}, s32[]{:T(128)}, bf16[4096,512]{1,0:T(8,128)(2,1)}, bf16[128,4,8,64]{0,3,2,1:T(8,128)(2,1)}) %tuple.27), branch_computations={%region_12.13_spmd, %region_13.15_spmd} | conditional | flops 4363124736 | bytes 158360080 | solution.py:67
  292.7 6.4 %copy.51 = bf16[4096,512]{0,1:T(8,128)(2,1)} copy(bf16[4096,512]{1,0:T(8,128)(2,1)} %get-tuple-element.56) | data formatting | bytes 8388608 | tf_op jit(solution)/shard_map
  299.1 2.7 fusion.56
  301.8 2.7 fusion.14
  304.6 24.5 %fusion.9 = (f32[4,8,128]{2,1,0:T(8,128)S(1)}, f32[4,4096,128,8]{2,1,3,0:T(8,128)}) fusion(pred[128,4096]{0,1:T(8,128)(4,1)S(1)} %fusion.14, bf16[4096,4,64,1]{0,2,3,1:T(8,128)(2,1)S(1)} %bitcast.118, bf16[128,4,8,64]{0,3,2,1:T(8,128)(2,1)} %get-tuple-element.23), kind=kOutput, calls=%fused_computation.12 | convolution fusion | flops 2181033984 | bytes 70270976 | tf_op jit(solution)/shard_map/cond/branch_1_fun/tkgd,ukd->kgtu/dot_general | solution.py:55
  329.1 24.2 %fusion.10 = f32[4,8,128,64]{2,3,1,0:T(8,128)} fusion(bf16[4096,4,64,1]{0,2,3,1:T(8,128)(2,1)S(1)} %bitcast.120, f32[4,4096,128,8]{2,1,3,0:T(8,128)} %get-tuple-element.67, pred[128,4096]{0,1:T(8,128)(4,1)S(1)} %fusion.14), kind=kOutput, calls=%fused_computation.13 | convolution fusion | flops 2181038080 | bytes 70778880 | tf_op jit(solution)/shard_map/cond/branch_1_fun/kgtu,ukd->kgtd/dot_general | solution.py:58
  353.2 1.4 divide_convert_fusion
  354.6 4.8 %multiply_reduce_fusion = (f32[128]{0:T(128)S(1)}, f32[128,2048]{1,0:T(8,128)S(1)}) fusion(bf16[128,2048]{0,1:T(8,128)(2,1)S(1)} %bitcast.123, bf16[1,2048,2048]{2,1,0:T(8,128)(2,1)} %all-gather.9.cloned.1.call-done, bf16[128,2048]{1,0:T(8,128)(2,1)} %copy-done.1), kind=kOutput, calls=%fused_computation.41 | convolution fusion | flops 1074790272 | bytes 10486272 | tf_op jit(solution)/shard_map/dot_general | solution.py:472
  359.4 1.0 copy-done.2
  360.4 0.9 multiply_convert_fusion.x_ref
  361.3 93.1 %shard_map.132 = bf16[128,2048]{1,0:T(8,128)(2,1)} custom-call(bf16[128,2048]{1,0:T(8,128)(2,1)} %multiply_convert_fusion.x_ref, f32[128,2048]{1,0:T(8,128)} %copy-done.2, f32[128,128]{1,0:T(8,128)} %pad_maximum_fusion.3.info_ref, bf16[2,2048,1536]{2,1,0:T(8,128)(2,1)} %bitcast.140, bf16[2,768,2048]{2,1,0:T(8,128)(2,1)} %bitcast.142), custom_call_target="tpu_custom_call" | custom-call | flops 12000000000 | bytes 20000000 | tf_op jit(solution)/shard_map/pallas_call | solution.py:402
  454.5 1.9 copy.68
  456.4 1.9 copy.69
  (60 shorter events, 0.4 us)
Async XLA Ops:
  7.2 8.7 %copy-start.5 = (f32[1,2048]{1,0:T(1,128)S(1)}, f32[1,2048]{1,0:T(1,128)}, u32[]{:S(2)}) copy-start(f32[1,2048]{1,0:T(1,128)} %param.18) | copy-start | bytes 24580
  7.2 11.8 %copy-start.12 = (s32[1,2,128,8]{2,3,1,0:T(8,128)S(1)}, s32[1,2,128,8]{2,3,1,0:T(8,128)}, u32[]{:S(2)}) copy-start(s32[1,2,128,8]{2,3,1,0:T(8,128)} %param.26) | copy-start | bytes 24580
  7.2 12.5 %copy-start.13 = (s32[1,2,128,8]{2,3,1,0:T(8,128)S(1)}, s32[1,2,128,8]{2,3,1,0:T(8,128)}, u32[]{:S(2)}) copy-start(s32[1,2,128,8]{2,3,1,0:T(8,128)} %param.27) | copy-start | bytes 24580
  7.2 14.4 %copy-start.14 = (f32[1,64]{1,0:T(1,128)S(1)}, f32[1,64]{1,0:T(1,128)}, u32[]{:S(2)}) copy-start(f32[1,64]{1,0:T(1,128)} %param.19) | copy-start | bytes 772
  7.2 53.6 %all-gather.5.cloned.1.call-start = ((), (), s32[]{:S(2)}) async-start(), calls=%async_computation | async-start | bytes 4325376 | tf_op jit(solution)/shard_map/all_gather | solution.py:47
  11.8 1.5 copy-start.10
  12.5 114.6 %all-gather.9.cloned.1.call-start = ((), (), s32[]{:S(2)}) async-start(), calls=%async_computation.2 | async-start | bytes 8650752 | tf_op jit(solution)/shard_map/all_gather | solution.py:466
  13.3 279.4 %all-gather.7.cloned.1.call-start = ((), (), s32[]{:S(2)}) async-start(), calls=%async_computation.1 | async-start | bytes 4325376 | tf_op jit(solution)/shard_map/all_gather | solution.py:47
  19.0 41.8 %copy-start.16 = (s32[128]{0:T(128)}, s32[128]{0:T(128)S(1)}, u32[]{:S(2)}) copy-start(s32[128]{0:T(128)S(1)} %iota_add_fusion) | copy-start | bytes 1540
  60.8 66.4 %copy-start = (bf16[1,128,2048]{2,1,0:T(8,128)(2,1)S(1)}, bf16[1,128,2048]{2,1,0:T(8,128)(2,1)}, u32[]{:S(2)}) copy-start(bf16[1,128,2048]{2,1,0:T(8,128)(2,1)} %param.16) | copy-start | bytes 1572868
  67.2 6.8 %copy-start.4 = (bf16[128,4,8,64]{0,3,2,1:T(8,128)(2,1)S(1)}, bf16[128,4,8,64]{0,3,2,1:T(8,128)(2,1)}, u32[]{:S(2)}) copy-start(bf16[128,4,8,64]{0,3,2,1:T(8,128)(2,1)} %get-tuple-element.19) | copy-start | bytes 1572868 | tf_op jit(solution)/shard_map/cond
  127.2 5.8 %copy-start.8 = (f32[1,2048]{1,0:T(1,128)S(1)}, f32[1,2048]{1,0:T(1,128)}, u32[]{:S(2)}) copy-start(f32[1,2048]{1,0:T(1,128)} %param.23) | copy-start | bytes 24580
  131.9 1.0 copy-start.3
  226.9 19.4 %copy-start.11 = (pred[128,64]{0,1:T(8,128)(4,1)S(1)}, pred[128,64]{0,1:T(8,128)(4,1)}, u32[]{:S(2)}) copy-start(pred[128,64]{0,1:T(8,128)(4,1)} %get-tuple-element.80) | copy-start | bytes 24580
  226.9 19.4 %copy-start.17 = (s32[128]{0:T(128)S(1)}, s32[128]{0:T(128)}, u32[]{:S(2)}) copy-start(s32[128]{0:T(128)} %copy-done.16) | copy-start | bytes 1540
  227.0 19.6 %copy-start.7 = (f32[128,64]{0,1:T(8,128)S(1)}, f32[128,64]{0,1:T(8,128)}, u32[]{:S(2)}) copy-start(f32[128,64]{0,1:T(8,128)} %get-tuple-element.78) | copy-start | bytes 98308
  227.0 20.2 %copy-start.6 = (f32[1,2048]{1,0:T(1,128)S(1)}, f32[1,2048]{1,0:T(1,128)}, u32[]{:S(2)}) copy-start(f32[1,2048]{1,0:T(1,128)} %param.18) | copy-start | bytes 24580
  227.0 14.0 %collective-permute-start = (bf16[128,2048]{1,0:T(8,128)(2,1)}, bf16[128,2048]{1,0:T(8,128)(2,1)S(1)}, u32[]{:S(2)}, u32[]{:S(2)}) collective-permute-start(bf16[128,2048]{1,0:T(8,128)(2,1)} %shard_map.131), channel_id=1, source_target_pairs={{0,32},{32,64},{64,96},{1,33},{33,65},{65,97},{2,34},{34,66},{66,9... | collective-permute-start | bytes 1572872 | tf_op jit(solution)/shard_map/ppermute | solution.py:21
  242.3 8.1 %copy-start.1 = (bf16[128,2048]{1,0:T(8,128)(2,1)}, bf16[128,2048]{1,0:T(8,128)(2,1)S(1)}, u32[]{:S(2)}) copy-start(bf16[128,2048]{1,0:T(8,128)(2,1)S(1)} %get-tuple-element.59) | copy-start | bytes 1572868
  242.3 8.1 %copy-start.15 = (f32[1,64]{1,0:T(1,128)S(1)}, f32[1,64]{1,0:T(1,128)}, u32[]{:S(2)}) copy-start(f32[1,64]{1,0:T(1,128)} %param.19) | copy-start | bytes 772
  354.6 5.8 %copy-start.9 = (f32[1,2048]{1,0:T(1,128)S(1)}, f32[1,2048]{1,0:T(1,128)}, u32[]{:S(2)}) copy-start(f32[1,2048]{1,0:T(1,128)} %param.23) | copy-start | bytes 24580
  359.4 1.0 copy-start.2
Sparse Core Ops, SparseCore 0:
  12.7 48.0 all-gather.4
  63.0 52.2 all-gather.8
  246.4 46.1 all-gather.6

commit v2 on v1

--- a/solution.py
+++ b/solution.py
@@ -1,4 +1,6 @@
 import functools
+import math
+
 import jax
 import jax.numpy as jnp
 from jax import lax
@@ -10,69 +12,22 @@
 QH = 32
 KVH = 4
 TOPK = 8
-
-
 EPS = 1e-06
-
-
-def shifted(x, axis, by):
-    peers = lax.axis_size(axis)
-    pairs = [(i, i + by) for i in range(peers) if 0 <= i + by < peers]
-    return lax.ppermute(x, axis, pairs)
-
-
-def rms_scale(values, gain):
-    mean_sq = jnp.mean(values * values, axis=-1, keepdims=True)
-    return values * lax.rsqrt(mean_sq + EPS) * gain
-
-
-def attend(attn_in, q_gain, k_gain, kv_w, place, seq_len):
-    tok = attn_in.shape[0]
-    kdim = KVH * HEAD
-    group = QH // KVH
-    kv_raw = jnp.dot(attn_in, kv_w, preferred_element_type=jnp.float32)
-    keys = rms_scale(kv_raw[:, :kdim].reshape(tok, KVH, HEAD), k_gain).reshape(tok, kdim)
-    keys_values = jnp.concatenate([keys, kv_raw[:, kdim:]], axis=1).astype(jnp.bfloat16)
-    queries = (
-        rms_scale(attn_in.astype(jnp.float32).reshape(tok, QH, HEAD), q_gain) * HEAD ** (-0.5)
-    ).astype(jnp.bfloat16)
-    queries = queries.reshape(tok, KVH, group, HEAD)
-    first_row = place * tok
-    qpos = first_row + jnp.arange(tok, dtype=jnp.int32)
-    seq_first = first_row // seq_len * seq_len
-    empty = (
-        jnp.zeros((KVH, group, tok), jnp.float32),
-        jnp.zeros((KVH, group, tok, HEAD), jnp.float32),
-    )
-    piece = lax.all_gather(keys_values, "expert", axis=0, tiled=True)
-    start = jnp.int32(0)
-    rows = piece.shape[0]
-
-    def accumulate(state):
-        kpos = jnp.arange(rows, dtype=jnp.int32)
-        key_rows = piece[:, :kdim].reshape(rows, KVH, HEAD)
-        value_rows = piece[:, kdim:].reshape(rows, KVH, HEAD)
-        scores = jnp.einsum("tkgd,ukd->kgtu", queries, key_rows, preferred_element_type=jnp.float32)
-        allowed = (kpos[None, :] <= qpos[:, None]) & (kpos[None, :] >= seq_first)
-        expw = jnp.where(allowed, jnp.exp(scores), 0.0)
-        mixed = jnp.einsum(
-            "kgtu,ukd->kgtd",
-            expw.astype(jnp.bfloat16),
-            value_rows,
-            preferred_element_type=jnp.float32,
-        )
-        return (jnp.sum(expw, axis=-1), mixed)
-
-    needed = (start <= qpos[tok - 1]) & (start + rows > seq_first)
-    total, mixed = lax.cond(needed, accumulate, lambda state: state, empty)
-    out = mixed / total[..., None]
-    return out.transpose(2, 0, 1, 3).reshape(tok, QH * HEAD).astype(jnp.bfloat16)
-
-
 MESH = pl.DeviceIdType.MESH
 CHUNKS = 4
 BF16 = jnp.bfloat16
 F32 = jnp.float32
+
+
+def each(n, first=0):
+    def wrap(f):
+        def step(i, carry):
+            f(i)
+            return carry
+
+        lax.fori_loop(first, n, step, 0)
+
+    return wrap
 
 
 def route_info(ids, weight_ints, experts_all):
@@ -86,14 +41,238 @@
     return jnp.concatenate([jnp.where(member, rank, -1.0).T, weight.T], axis=0)
 
 
+def rms_scale(values, gain):
+    mean_sq = jnp.mean(values * values, axis=-1, keepdims=True)
+    return values * lax.rsqrt(mean_sq + EPS) * gain
+
+
+def attn_kernel(
+    h_ref, gain_ref, qgain_ref, kgain_ref, kvw_ref, out_ref, kv, qs, acc, s1, s2, s3, rk
+):
+    me = lax.axis_index("expert")
+    sec = lax.axis_index("section")
+    y, z, c = me // 8, (me // 2) % 4, me % 2
+    g = c * z + (1 - c) * y
+    ln = c * y + (1 - c) * z
+    tok = h_ref.shape[0]
+    kdim = KVH * HEAD
+    group = QH // KVH
+
+    def peer(gp, lp):
+        return 2 * (c * (4 * lp + gp) + (1 - c) * (4 * gp + lp)) + c
+
+    sibling = me + 1 - 2 * c
+
+    def remote(block, send, dev):
+        return pltpu.make_async_remote_copy(
+            src_ref=kv.at[block],
+            dst_ref=kv.at[block],
+            send_sem=send,
+            recv_sem=rk.at[block],
+            device_id=(sec, dev),
+            device_id_type=MESH,
+        )
+
+    def gather_copy(k):
+        return remote(me, s1.at[k], peer((g + k) % 4, ln))
+
+    def line_copy(gp, k):
+        return remote(peer(gp, ln), s2.at[4 * gp + k], peer(g, (ln + k) % 4))
+
+    def pair_copy(gp, lp):
+        return remote(peer(gp, lp), s3.at[4 * gp + lp], sibling)
+
+    def arrival(block):
+        return remote(block, s1.at[0], sibling)
+
+    barrier = pltpu.get_barrier_semaphore()
+
+    def greet(dev):
+        pl.semaphore_signal(barrier, inc=1, device_id=(sec, dev), device_id_type=MESH)
+
+    @each(4, 1)
+    def _(k):
+        greet(peer((g + k) % 4, ln))
+        greet(peer(g, (ln + k) % 4))
+
+    greet(sibling)
+
+    r0 = lax.broadcasted_iota(jnp.int32, (256, 256), 0) // HEAD
+    c0 = lax.broadcasted_iota(jnp.int32, (256, 256), 1) // HEAD
+    averager = jnp.where(r0 == c0, 1.0 / HEAD, 0.0).astype(BF16)
+
+    def head_means(x):
+        sq = x * x
+        high = sq.astype(BF16)
+        low = (sq - high.astype(F32)).astype(BF16)
+        return jnp.dot(high, averager, preferred_element_type=F32) + jnp.dot(
+            low, averager, preferred_element_type=F32
+        )
+
+    h32 = h_ref[...].astype(F32)
+    scale = lax.rsqrt(jnp.mean(h32 * h32, axis=-1, keepdims=True) + EPS)
+    attn_in = (h32 * scale * gain_ref[...]).astype(BF16)
+    kv_raw = jnp.dot(attn_in, kvw_ref[...], preferred_element_type=F32)
+    keys = kv_raw[:, :kdim]
+    keys = keys * lax.rsqrt(head_means(keys) + EPS) * kgain_ref[...]
+    kv[me] = jnp.concatenate([keys, kv_raw[:, kdim:]], axis=1).astype(BF16)
+
+    pl.semaphore_wait(barrier, 7)
+
+    @each(4, 1)
+    def _(k):
+        gather_copy(k).start()
+
+    @each(4, 1)
+    def _(k):
+        line_copy(g, k).start()
+
+    pair_copy(g, ln).start()
+
+    low_half = lax.broadcasted_iota(jnp.int32, (tok, 128), 1) < HEAD
+    for t in range(QH * HEAD // 256):
+        part = attn_in[:, 256 * t : 256 * t + 256].astype(F32)
+        query = part * lax.rsqrt(head_means(part) + EPS) * qgain_ref[:, 256 * t : 256 * t + 256]
+        for n in range(4):
+            head = 4 * t + n
+            at = (head // group) % 2
+            tile = query[:, 128 * (n // 2) : 128 * (n // 2) + 128]
+            if n % 2 != at:
+                tile = pltpu.roll(tile, HEAD, 1)
+            tile = jnp.where(low_half == (at == 0), tile, 0.0)
+            first = head % group * tok
+            qs[head // group, first : first + tok, :] = tile.astype(BF16)
+
+    @each(4, 1)
+    def _(k):
+        gp = (g + k) % 4
+        arrival(peer(gp, ln)).wait_recv()
+
+        @each(4, 1)
+        def _(m):
+            line_copy(gp, m).start()
+
+        pair_copy(gp, ln).start()
+
+    @each(4)
+    def _(m):
+        gp = (g + m) % 4
+
+        @each(4, 1)
+        def _(k):
+            lp = (ln + k) % 4
+            arrival(peer(gp, lp)).wait_recv()
+            pair_copy(gp, lp).start()
+
+    @each(16)
+    def _(n):
+        arrival(2 * n + 1 - c).wait_recv()
+
+    span = 4 * tok
+    ones = jnp.ones((span, 128), BF16)
+    last = me // 4
+    rows = group * tok
+    qpos = me * tok + lax.broadcasted_iota(jnp.int32, (rows, span), 0) % tok
+    upos = lax.broadcasted_iota(jnp.int32, (rows, span), 1)
+
+    @each(KVH // 2)
+    def _(pair):
+        kcols = pl.ds(pl.multiple_of(pair * 128, 128), 128)
+        vcols = pl.ds(pl.multiple_of(kdim + pair * 128, 128), 128)
+        for at in range(2):
+
+            def step(kb, masked):
+                keys = kv[pl.ds(4 * kb, 4), :, kcols].reshape(span, 128)
+                values = kv[pl.ds(4 * kb, 4), :, vcols].reshape(span, 128)
+                score = lax.dot_general(
+                    qs[2 * pair + at],
+                    keys,
+                    (((1,), (1,)), ((), ())),
+                    preferred_element_type=F32,
+                )
+                expw = jnp.exp2(score)
+                if masked:
+                    expw = jnp.where(upos + kb * span <= qpos, expw, 0.0)
+                return jnp.dot(
+                    expw.astype(BF16),
+                    jnp.concatenate([values, ones], axis=1),
+                    preferred_element_type=F32,
+                )
+
+            acc[...] = step(last, True)
+
+            def body(kb, carry):
+                acc[...] += step(kb, False)
+                return carry
+
+            lax.fori_loop(0, last, body, 0)
+            mixed = acc[:, :128] / acc[:, 128:]
+            for n in range(group // 2):
+                even = mixed[2 * n * tok : (2 * n + 1) * tok]
+                odd = mixed[(2 * n + 1) * tok : (2 * n + 2) * tok]
+                if at == 0:
+                    odd = pltpu.roll(odd, HEAD, 1)
+                else:
+                    even = pltpu.roll(even, HEAD, 1)
+                first = pl.multiple_of((2 * pair + at) * (group // 2) * 128 + n * 128, 128)
+                out_ref[:, pl.ds(first, 128)] = jnp.where(low_half, even, odd).astype(BF16)
+
+    @each(4, 1)
+    def _(k):
+        gather_copy(k).wait_send()
+
+    @each(4)
+    def _(gp):
+        @each(4, 1)
+        def _(k):
+            line_copy(gp, k).wait_send()
+
+        @each(4)
+        def _(lp):
+            pair_copy(gp, lp).wait_send()
+
+
+def attend(hidden, attn_gain, q_gain, k_gain, kv_w, tick):
+    tok, d = hidden.shape
+    vmem = pl.BlockSpec(memory_space=pltpu.VMEM)
+    dma = pltpu.SemaphoreType.DMA
+    qscale = jnp.tile(q_gain * (HEAD**-0.5 * math.log2(math.e)), QH)[None]
+    return pl.pallas_call(
+        attn_kernel,
+        out_shape=jax.ShapeDtypeStruct((tok, d), BF16),
+        in_specs=[vmem] * 5,
+        out_specs=vmem,
+        scratch_shapes=[
+            pltpu.VMEM((32, tok, 2 * KVH * HEAD), BF16),
+            pltpu.VMEM((KVH, QH // KVH * tok, 128), BF16),
+            pltpu.VMEM((QH // KVH * tok, 256), F32),
+            dma((4,)),
+            dma((16,)),
+            dma((16,)),
+            dma((32,)),
+        ],
+        compiler_params=pltpu.CompilerParams(
+            collective_id=2 + tick, has_side_effects=True, vmem_limit_bytes=56 << 20
+        ),
+        cost_estimate=pl.CostEstimate(
+            flops=40 * 10**9, bytes_accessed=20 * 10**6, transcendentals=10**6
+        ),
+    )(hidden, attn_gain[None], qscale, jnp.tile(k_gain, KVH)[None], kv_w)
+
+
 def moe_kernel(
     cap,
-    x_ref,
-    after_ref,
-    info_ref,
-    gu_hbm,
-    dn_hbm,
-    out_ref,
+    passes,
+    *refs,
+):
+    if passes:
+        x_ref, after_ref, info_ref, gu_hbm, dn_hbm, fresh_ref, out_ref, next_ref = refs[:8]
+        ob, nb, s5, r5 = refs[-4:]
+        refs = refs[8:-4]
+    else:
+        x_ref, after_ref, info_ref, gu_hbm, dn_hbm, out_ref = refs[:6]
+        refs = refs[6:]
+    (
     xg,
     sb,
     xb,
@@ -121,7 +300,7 @@
     s4,
     r4,
     wsem,
-):
+    ) = refs
     me = lax.axis_index("expert")
     sec = lax.axis_index("section")
     y, z, c = me // 8, (me // 2) % 4, me % 2
@@ -194,15 +373,15 @@
         gp = (g + k) % 4
         return remote(pr.at[j, gp], pr.at[j, gp], s4.at[j, k], r4.at[j, gp], relay(gp))
 
-    def each(n, first=0):
-        def wrap(f):
-            def step(i, carry):
-                f(i)
-                return carry
-
-            lax.fori_loop(first, n, step, 0)
-
-        return wrap
+    def next_copy(j):
+        return pltpu.make_async_remote_copy(
+            src_ref=ob.at[j],
+            dst_ref=nb.at[j],
+            send_sem=s5.at[j],
+            recv_sem=r5.at[j],
+            device_id=((sec + 1) % 4, me),
+            device_id_type=MESH,
+        )
 
     gu_copy = pltpu.make_async_copy(gu_hbm, gu, wsem.at[0])
     dn_copy = pltpu.make_async_copy(dn_hbm, dn, wsem.at[1])
@@ -220,11 +399,17 @@
     def _(k):
         greet(8 * ((y + k) % 4) + 2 * z)
         greet(8 * ((y + k) % 4) + 2 * z + 1)
+
+    if passes:
+        for by in (1, 3):
+            pl.semaphore_signal(
+                barrier, inc=1, device_id=((sec + by) % 4, me), device_id_type=MESH
+            )
 
     infog[g] = info_ref[...]
     for j in range(chunks):
         xg[j, g] = x_ref[:, j * width : (j + 1) * width]
-    pl.semaphore_wait(barrier, 13)
+    pl.semaphore_wait(barrier, 15 if passes else 13)
 
     @each(4, 1)
     def _(k):
@@ -372,7 +557,19 @@
             sum_arrival(j, k).wait_recv()
             tot[:, at] += pr[j, (g + k) % 4].astype(F32)
 
-        out_ref[:, at] = tot[:, at].astype(BF16)
+        made = tot[:, at].astype(BF16)
+        out_ref[:, at] = made
+        if passes:
+            ob[j] = made
+            next_copy(j).start()
+
+    if passes:
+
+        @each(chunks)
+        def _(j):
+            at = pl.ds(pl.multiple_of(j * width, width), width)
+            next_copy(j).wait()
+            next_ref[:, at] = jnp.where(sec == 0, fresh_ref[:, at], nb[j])
 
     @each(4, 1)
     def _(k):
@@ -391,7 +588,7 @@
             back_copy(j, (my_slot + k) % 8).wait_send()
 
 
-def moe_layer(moe_in, after_attn, info, gate_up, down, cap, tick):
+def moe_layer(moe_in, after_attn, info, gate_up, down, cap, tick, fresh):
     tok, d = moe_in.shape
     ff = down.shape[1]
     w = d // CHUNKS
@@ -399,11 +596,19 @@
     vmem = pl.BlockSpec(memory_space=pltpu.VMEM)
     hbm = pl.BlockSpec(memory_space=pl.ANY)
     dma = pltpu.SemaphoreType.DMA
+    passes = fresh is not None
+    outs = 2 if passes else 1
+    handed = [
+        pltpu.VMEM((CHUNKS, tok, w), BF16),
+        pltpu.VMEM((CHUNKS, tok, w), BF16),
+        dma((CHUNKS,)),
+        dma((CHUNKS,)),
+    ]
     return pl.pallas_call(
-        functools.partial(moe_kernel, cap),
-        out_shape=jax.ShapeDtypeStruct((tok, d), BF16),
-        in_specs=[vmem, vmem, vmem, hbm, hbm],
-        out_specs=vmem,
+        functools.partial(moe_kernel, cap, passes),
+        out_shape=[jax.ShapeDtypeStruct((tok, d), BF16)] * outs,
+        in_specs=[vmem, vmem, vmem, hbm, hbm] + [vmem] * passes,
+        out_specs=[vmem] * outs,
         scratch_shapes=[
             pltpu.VMEM((CHUNKS, 4, tok, w), BF16),
             pltpu.VMEM((CHUNKS, 8, rows, w), BF16),
@@ -432,14 +637,15 @@
             dma((CHUNKS, 4)),
             dma((CHUNKS, 4)),
             dma((2,)),
-        ],
+        ]
+        + handed * passes,
         compiler_params=pltpu.CompilerParams(
             collective_id=4 + tick, has_side_effects=True, vmem_limit_bytes=64 << 20
         ),
         cost_estimate=pl.CostEstimate(
             flops=12 * 10**9, bytes_accessed=20 * 10**6, transcendentals=10**6
         ),
-    )(moe_in, after_attn, info, gate_up, down)
+    )(moe_in, after_attn, info, gate_up, down, *([fresh] if passes else []))
 
 
 def body(
@@ -457,28 +663,23 @@
     route_weights,
 ):
     devices = lax.axis_size("expert")
-    place = lax.axis_index("expert")
     tok = section_input.shape[1]
     experts_all = expert_gate_up.shape[1] * devices
     cap = tok * TOPK * 9 // (8 * experts_all)
-    seq_len = tok * devices
     infos = [route_info(route_ids[0, t], route_weights[0, t], experts_all) for t in range(2)]
     out_full = lax.all_gather(out_weight[0], "expert", axis=0, tiled=True)
 
-    def layer(hidden, tick):
-        h32 = hidden.astype(jnp.float32)
-        attn_in = rms_scale(h32, attn_gain[0]).astype(jnp.bfloat16)
-        attended = attend(attn_in, query_gain[0], key_gain[0], kv_weight[0], place, seq_len)
-        after_attn = h32 + jnp.dot(attended, out_full, preferred_element_type=jnp.float32)
-        moe_in = rms_scale(after_attn, moe_gain[0]).astype(jnp.bfloat16)
+    def layer(hidden, tick, fresh):
+        h32 = hidden.astype(F32)
+        attended = attend(hidden, attn_gain[0], query_gain[0], key_gain[0], kv_weight[0], tick)
+        after_attn = h32 + jnp.dot(attended, out_full, preferred_element_type=F32)
+        moe_in = rms_scale(after_attn, moe_gain[0]).astype(BF16)
         return moe_layer(
-            moe_in, after_attn, infos[tick], expert_gate_up[0], expert_down[0], cap, tick
+            moe_in, after_attn, infos[tick], expert_gate_up[0], expert_down[0], cap, tick, fresh
         )
 
-    first_out = layer(section_input[0], 0)
-    incoming = shifted(first_out, "section", 1)
-    second_in = jnp.where(lax.axis_index("section") == 0, fresh_batch, incoming)
-    second_out = layer(second_in, 1)
+    first_out, second_in = layer(section_input[0], 0, fresh_batch)
+    (second_out,) = layer(second_in, 1, None)
     return (first_out[None], second_out[None])
 
 

time: 468 us -> 343 us (0.73)
  matrix products: 115 us -> 10.3 us
  Pallas kernels: 186 us -> 281 us
  waiting for transfers between devices: 90.5 us -> 21.4 us
  local copies, waits for them, and re-layouts: 32 us -> 8.47 us
  other arithmetic: 22.7 us -> 4.72 us
    dot_general x8 -> x2, matrix products: 114 us -> 9.92 us  [layer(): after_attn = h32 + jnp.dot(attended, out_full, preferred_element_type=F32)]
    pallas_call x2 -> x4, Pallas kernels: 186 us -> 281 us  [the longest x2 220 us: moe_layer(): pl.pallas_call(functools.partial(moe_kernel, cap, passes), out_shape=[jax...]
    all_gather x2 -> x0, waiting for transfers between devices: 79.2 us -> none  [attend(): piece = lax.all_gather(keys_values, 'expert', axis=0, tiled=True)]
    all_gather x1, waiting for transfers between devices: 0.02 us -> 20.7 us  [body(): out_full = lax.all_gather(out_weight[0], 'expert', axis=0, tiled=True)]
    another operation x2 -> x4, local copies, waits for them, and re-layouts: 12.9 us -> 1.95 us  [the longest x2 1.27 us: attend(): jnp.tile(k_gain, KVH)[None]]
    ppermute x1 -> x0, waiting for transfers between devices: 10.6 us -> none  [shifted(): return lax.ppermute(x, axis, pairs)]
    slice x5 -> x0, local copies, waits for them, and re-layouts: 7.97 us -> none  [the longest x2 6.76 us: accumulate(): value_rows = piece[:, kdim:].reshape(rows, KVH, HEAD)]
    and x2 -> x0, other arithmetic: 5.48 us -> none  [accumulate(): allowed = (kpos[None, :] <= qpos[:, None]) & (kpos[None, :] >= seq_first)]
  transfers between devices with their start and end apart: 4 -> 1, of which waited for: 3 -> 1; matrix products, arithmetic and copies ran while one was open for 17% -> 2% of each run, Pallas kernels for 0% -> 10%
where the time goes in v2:
time: 343 us; the launch traced here: 340 us
  Pallas kernels  281 us (82%)
  waiting for transfers between devices  21.4 us (6%)
  between operations  14.1 us (4%)
  matrix products  10.3 us (3%)
  local copies, waits for them, and re-layouts  8.47 us (2%)
  other arithmetic  4.72 us (1%)
    pallas_call x2, Pallas kernels, moe_layer(): pl.pallas_call(functools.partial(moe_kernel, cap, passes), out_shape=[jax...  220 us
    pallas_call x2, Pallas kernels, attend(): pl.pallas_call(attn_kernel, out_shape=jax.ShapeDtypeStruct((tok, d), BF16...  61.4 us
    all_gather x1, waiting for transfers between devices, body(): out_full = lax.all_gather(out_weight[0], 'expert', axis=0, tiled=True)  20.7 us
    dot_general x2, matrix products, layer(): after_attn = h32 + jnp.dot(attended, out_full, preferred_element_type=F32)  9.92 us
  transfers between devices with their start and end apart: 1, of which 1 were waited for; matrix products, arithmetic and copies ran while one was open for 2% of the time, Pallas kernels for 10%

profile of v2, /device:TPU:32, one launch (start us, length us, event | category | flops | bytes accessed | tf_op | source)
XLA Modules:
  0.0 340.3 jit_solution(3075999944665381513)
XLA Ops:
  7.2 0.0 all-gather.3.cloned.1.call-start
  7.2 0.7 all-gather.3.cloned.1.call-update
  7.9 0.7 multiply_bitcast_fusion.2
  8.6 0.7 broadcast_in_dim_tile.8.qgain_ref
  9.2 0.7 tile.11
  9.9 0.6 broadcast_in_dim_tile.9.kgain_ref
  10.5 0.7 slice_bitcast_fusion
  11.2 0.1 fusion.10
  11.3 0.7 multiply_bitcast_fusion
  12.0 0.1 select_reduce_fusion
  12.1 0.2 convolution_select_fusion.1
  12.3 0.7 pad_maximum_fusion.refs_2_
  12.9 0.2 convolution_select_fusion
  13.1 0.6 pad_maximum_fusion.1.refs_2_
  13.8 0.0 copy-start.2
  13.8 33.1 %shard_map.131 = bf16[128,2048]{1,0:T(8,128)(2,1)} custom-call(bf16[128,2048]{1,0:T(8,128)(2,1)} %bitcast.42, f32[1,2048]{1,0:T(1,128)} %gain_ref.3, f32[1,2048]{1,0:T(1,128)} %broadcast_in_dim_tile.8.qgain_ref, f32[1,256]{1,0:T(1,128)} %broadcast_in_dim_tile.9.kgain_ref, bf16[2048,512]{1,0:T(8,128)(2,1)} %bitcast.54), custom_call_target="tpu_custom_call" | custom-call | flops 40000000000 | bytes 20000000 | tf_op jit(solution)/shard_map/pallas_call | solution.py:240
  46.8 0.0 copy-start.4
  46.8 20.7 %all-gather.3.cloned.1.call-done = bf16[1,2048,2048]{2,1,0:T(8,128)(2,1)} async-done(((bf16[1,64,2048]{2,1,0:T(8,128)(2,1)}), bf16[1,2048,2048]{2,1,0:T(8,128)(2,1)}) %all-gather.3.cloned.1.call-update) | async-done | bytes 8388624 | tf_op jit(solution)/shard_map/all_gather | solution.py:670
  67.6 0.0 copy-done.2
  67.6 5.0 %multiply_reduce_fusion.1 = (f32[128]{0:T(128)S(1)}, f32[128,2048]{1,0:T(8,128)S(1)}) fusion(bf16[128,2048]{1,0:T(8,128)(2,1)} %shard_map.131, bf16[1,2048,2048]{2,1,0:T(8,128)(2,1)} %all-gather.3.cloned.1.call-done, bf16[1,128,2048]{2,1,0:T(8,128)(2,1)S(1)} %copy-done.2), kind=kOutput, calls=%fused_computation.11 | convolution fusion | flops 1074790272 | bytes 10486272 | tf_op jit(solution)/shard_map/dot_general | solution.py:675
  72.6 0.0 copy-start
  72.6 1.1 copy-done
  73.6 0.0 copy-done.4
  73.6 1.0 multiply_convert_fusion.1.refs_0_
  74.6 102.7 %shard_map.132 = (bf16[128,2048]{1,0:T(8,128)(2,1)}, bf16[128,2048]{1,0:T(8,128)(2,1)}) custom-call(bf16[128,2048]{1,0:T(8,128)(2,1)} %multiply_convert_fusion.1.refs_0_, f32[128,2048]{1,0:T(8,128)} %copy-done, f32[128,128]{1,0:T(8,128)} %pad_maximum_fusion.refs_2_, bf16[2,2048,1536]{2,1,0:T(8,128)(2,1)} %bitcast.50, bf16[2,768,2048]{2,1,0:T(8,128)(2,1)} %bitcast.52, ...), custom_call_target="tpu_custom_call" | custom-call | flops 12000000000 | bytes 20000000 | tf_op jit(solution)/shard_map/pallas_call | solution.py:607
  177.3 0.0 copy-start.3
  177.3 28.4 %shard_map.133 = bf16[128,2048]{1,0:T(8,128)(2,1)} custom-call(bf16[128,2048]{1,0:T(8,128)(2,1)} %get-tuple-element.5.h_ref, f32[1,2048]{1,0:T(1,128)} %gain_ref.3, f32[1,2048]{1,0:T(1,128)} %broadcast_in_dim_tile.8.qgain_ref, f32[1,256]{1,0:T(1,128)} %broadcast_in_dim_tile.9.kgain_ref, bf16[2048,512]{1,0:T(8,128)(2,1)} %bitcast.55), custom_call_target="tpu_custom_call" | custom-call | flops 40000000000 | bytes 20000000 | tf_op jit(solution)/shard_map/pallas_call | solution.py:240
  205.6 0.0 copy-done.3
  205.7 0.0 copy-start.5
  205.7 5.0 %multiply_reduce_fusion = (f32[128]{0:T(128)S(1)}, f32[128,2048]{1,0:T(8,128)S(1)}) fusion(bf16[128,2048]{1,0:T(8,128)(2,1)} %shard_map.133, bf16[1,2048,2048]{2,1,0:T(8,128)(2,1)} %all-gather.3.cloned.1.call-done, bf16[128,2048]{1,0:T(8,128)(2,1)S(1)} %copy-done.3), kind=kOutput, calls=%fused_computation.9 | convolution fusion | flops 1074790272 | bytes 10486272 | tf_op jit(solution)/shard_map/dot_general | solution.py:675
  210.6 0.0 copy-start.1
  210.7 1.0 copy-done.1
  211.6 0.0 copy-done.5
  211.6 0.9 multiply_convert_fusion.refs_0_
  212.6 117.1 %shard_map.134 = bf16[128,2048]{1,0:T(8,128)(2,1)} custom-call(bf16[128,2048]{1,0:T(8,128)(2,1)} %multiply_convert_fusion.refs_0_, f32[128,2048]{1,0:T(8,128)} %copy-done.1, f32[128,128]{1,0:T(8,128)} %pad_maximum_fusion.1.refs_2_, bf16[2,2048,1536]{2,1,0:T(8,128)(2,1)} %bitcast.51, bf16[2,768,2048]{2,1,0:T(8,128)(2,1)} %bitcast.53), custom_call_target="tpu_custom_call" | custom-call | flops 12000000000 | bytes 20000000 | tf_op jit(solution)/shard_map/pallas_call | solution.py:607
  329.7 1.9 copy.20
  331.6 1.9 copy.21
  (4 shorter events, 0.0 us)
Async XLA Ops:
  7.2 60.4 %all-gather.3.cloned.1.call-start = ((), (), s32[]{:S(2)}) async-start(), calls=%async_computation | async-start | bytes 8650752 | tf_op jit(solution)/shard_map/all_gather | solution.py:670
  13.8 53.8 %copy-start.2 = (bf16[1,128,2048]{2,1,0:T(8,128)(2,1)S(1)}, bf16[1,128,2048]{2,1,0:T(8,128)(2,1)}, u32[]{:S(2)}) copy-start(bf16[1,128,2048]{2,1,0:T(8,128)(2,1)} %param.12) | copy-start | bytes 1572868
  46.8 26.8 %copy-start.4 = (f32[1,2048]{1,0:T(1,128)S(1)}, f32[1,2048]{1,0:T(1,128)}, u32[]{:S(2)}) copy-start(f32[1,2048]{1,0:T(1,128)} %param.19) | copy-start | bytes 24580
  72.6 1.1 copy-start
  177.3 28.4 %copy-start.3 = (bf16[128,2048]{1,0:T(8,128)(2,1)S(1)}, bf16[128,2048]{1,0:T(8,128)(2,1)}, u32[]{:S(2)}) copy-start(bf16[128,2048]{1,0:T(8,128)(2,1)} %get-tuple-element.5.h_ref) | copy-start | bytes 1572868
  205.7 6.0 %copy-start.5 = (f32[1,2048]{1,0:T(1,128)S(1)}, f32[1,2048]{1,0:T(1,128)}, u32[]{:S(2)}) copy-start(f32[1,2048]{1,0:T(1,128)} %param.19) | copy-start | bytes 24580
  210.6 1.0 copy-start.1
Sparse Core Ops, SparseCore 0:
  10.3 57.2 all-gather.2

commit v3 on v2

--- a/solution.py
+++ b/solution.py
@@ -30,25 +30,131 @@
     return wrap
 
 
-def route_info(ids, weight_ints, experts_all):
-    chosen = ids[:, :, None] == jnp.arange(experts_all, dtype=jnp.int32)[None, None, :]
-    member = jnp.any(chosen, axis=1)
-    gates = weight_ints.astype(F32) * (1.0 / 1024.0)
-    weight = jnp.sum(jnp.where(chosen, gates[..., None], 0.0), axis=1)
-    tok = ids.shape[0]
-    before = jnp.tril(jnp.ones((tok, tok), BF16), -1)
-    rank = jnp.dot(before, member.astype(BF16), preferred_element_type=F32)
-    return jnp.concatenate([jnp.where(member, rank, -1.0).T, weight.T], axis=0)
-
-
-def rms_scale(values, gain):
-    mean_sq = jnp.mean(values * values, axis=-1, keepdims=True)
-    return values * lax.rsqrt(mean_sq + EPS) * gain
-
-
-def attn_kernel(
-    h_ref, gain_ref, qgain_ref, kgain_ref, kvw_ref, out_ref, kv, qs, acc, s1, s2, s3, rk
-):
+def route_info(ids, gates, experts_all):
+    topk, tok = ids.shape
+    expert = lax.broadcasted_iota(jnp.int32, (experts_all, tok), 0)
+    member = jnp.zeros((experts_all, tok), F32)
+    weight = jnp.zeros((experts_all, tok), F32)
+    for k in range(topk):
+        chosen = ids[k : k + 1] == expert
+        member += jnp.where(chosen, 1.0, 0.0)
+        weight += jnp.where(chosen, gates[k : k + 1], 0.0)
+    earlier = lax.broadcasted_iota(jnp.int32, (tok, tok), 0)
+    later = lax.broadcasted_iota(jnp.int32, (tok, tok), 1)
+    before = jnp.where(earlier < later, 1.0, 0.0).astype(BF16)
+    rank = jnp.dot(member.astype(BF16), before, preferred_element_type=F32)
+    return jnp.concatenate([jnp.where(member > 0.5, rank, -1.0), weight], axis=0)
+
+
+def silu(x):
+    half = 0.5 * x
+    return half + half * jnp.tanh(half)
+
+
+class Exchange:
+    def __init__(self, buf, s1, s2, sf, s3, rk, sec, c, g, ln, sibling):
+        self.buf, self.s1, self.s2, self.sf, self.s3, self.rk = buf, s1, s2, sf, s3, rk
+        self.sec, self.c, self.g, self.ln, self.sibling = sec, c, g, ln, sibling
+
+    def slot(self, t, lp, gp):
+        return (t * 4 + lp) * 4 + gp
+
+    def peer(self, lp, gp):
+        c = self.c
+        return 2 * (c * (4 * lp + gp) + (1 - c) * (4 * gp + lp)) + c
+
+    def copy(self, slot, send, dev):
+        return pltpu.make_async_remote_copy(
+            src_ref=self.buf.at[slot],
+            dst_ref=self.buf.at[slot],
+            send_sem=send,
+            recv_sem=self.rk.at[slot],
+            device_id=(self.sec, dev),
+            device_id_type=MESH,
+        )
+
+    def gather(self, k):
+        own = self.slot(self.c, self.ln, self.g)
+        return self.copy(own, self.s1.at[k], self.peer(self.ln, (self.g + k) % 4))
+
+    def along(self, gp, n):
+        to = self.peer((self.ln + 1 + 2 * n) % 4, self.g)
+        return self.copy(self.slot(self.c, self.ln, gp), self.s2.at[2 * gp + n], to)
+
+    def onward(self, gp):
+        by = 1 + 2 * (gp // 2)
+        source, to = (self.ln + 4 - by) % 4, (self.ln + by) % 4
+        return self.copy(self.slot(self.c, source, gp), self.sf.at[gp], self.peer(to, self.g))
+
+    def across(self, lp, gp):
+        return self.copy(self.slot(self.c, lp, gp), self.s3.at[4 * lp + gp], self.sibling)
+
+    def arrive(self, t, lp, gp):
+        self.copy(self.slot(t, lp, gp), self.s1.at[0], self.sibling).wait_recv()
+
+    def send_own(self):
+        @each(4, 1)
+        def _(k):
+            self.gather(k).start()
+
+        self.pass_on(self.g)
+
+    def pass_on(self, gp):
+        @each(2)
+        def _(n):
+            self.along(gp, n).start()
+
+        self.across(self.ln, gp).start()
+
+    def take_gathered(self):
+        @each(4, 1)
+        def _(k):
+            gp = (self.g + k) % 4
+            self.arrive(self.c, self.ln, gp)
+            self.pass_on(gp)
+
+    def take_line(self, by):
+        lp = (self.ln + by) % 4
+
+        @each(4)
+        def _(gp):
+            self.arrive(self.c, lp, gp)
+            self.across(lp, gp).start()
+
+            @pl.when(by * (1 - gp // 2) + (4 - by) * (gp // 2) == 3)
+            def _():
+                self.onward(gp).start()
+
+    def take_pair(self, lp):
+        @each(4)
+        def _(gp):
+            self.arrive(1 - self.c, lp, gp)
+
+    def finish(self):
+        @each(4, 1)
+        def _(k):
+            self.gather(k).wait_send()
+
+        @each(4)
+        def _(gp):
+            self.onward(gp).wait_send()
+
+            @each(2)
+            def _(n):
+                self.along(gp, n).wait_send()
+
+            @each(4)
+            def _(lp):
+                self.across(lp, gp).wait_send()
+
+
+def attn_kernel(gathers, *refs):
+    h_ref, gain_ref, qgain_ref, kgain_ref, kvw_ref, w_ref = refs[:6]
+    if gathers:
+        after_ref, w_out, kv, qs, acc, att, wf, wsem = refs[6:14]
+    else:
+        after_ref, kv, qs, acc, att, wf, wsem = refs[6:13]
+    sems = refs[14:] if gathers else refs[13:]
     me = lax.axis_index("expert")
     sec = lax.axis_index("section")
     y, z, c = me // 8, (me // 2) % 4, me % 2
@@ -57,33 +163,10 @@
     tok = h_ref.shape[0]
     kdim = KVH * HEAD
     group = QH // KVH
-
-    def peer(gp, lp):
-        return 2 * (c * (4 * lp + gp) + (1 - c) * (4 * gp + lp)) + c
-
+    rows = group * tok
+    span = 4 * tok
     sibling = me + 1 - 2 * c
-
-    def remote(block, send, dev):
-        return pltpu.make_async_remote_copy(
-            src_ref=kv.at[block],
-            dst_ref=kv.at[block],
-            send_sem=send,
-            recv_sem=rk.at[block],
-            device_id=(sec, dev),
-            device_id_type=MESH,
-        )
-
-    def gather_copy(k):
-        return remote(me, s1.at[k], peer((g + k) % 4, ln))
-
-    def line_copy(gp, k):
-        return remote(peer(gp, ln), s2.at[4 * gp + k], peer(g, (ln + k) % 4))
-
-    def pair_copy(gp, lp):
-        return remote(peer(gp, lp), s3.at[4 * gp + lp], sibling)
-
-    def arrival(block):
-        return remote(block, s1.at[0], sibling)
+    kvx = Exchange(kv, *sems[:5], sec, c, g, ln, sibling)
 
     barrier = pltpu.get_barrier_semaphore()
 
@@ -92,10 +175,17 @@
 
     @each(4, 1)
     def _(k):
-        greet(peer((g + k) % 4, ln))
-        greet(peer(g, (ln + k) % 4))
+        greet(kvx.peer(ln, (g + k) % 4))
+        greet(kvx.peer((ln + k) % 4, g))
 
     greet(sibling)
+    if gathers:
+        wx = Exchange(wf, *sems[5:10], sec, c, g, ln, sibling)
+        wf[wx.slot(c, ln, g)] = w_ref[...]
+        keep = pltpu.make_async_copy(wf, w_out, wsem)
+    else:
+        fetch = pltpu.make_async_copy(w_ref, wf, wsem)
+        fetch.start()
 
     r0 = lax.broadcasted_iota(jnp.int32, (256, 256), 0) // HEAD
     c0 = lax.broadcasted_iota(jnp.int32, (256, 256), 1) // HEAD
@@ -114,25 +204,18 @@
     attn_in = (h32 * scale * gain_ref[...]).astype(BF16)
     kv_raw = jnp.dot(attn_in, kvw_ref[...], preferred_element_type=F32)
     keys = kv_raw[:, :kdim]
-    keys = keys * lax.rsqrt(head_means(keys) + EPS) * kgain_ref[...]
-    kv[me] = jnp.concatenate([keys, kv_raw[:, kdim:]], axis=1).astype(BF16)
+    kgain = jnp.concatenate([kgain_ref[...]] * KVH, axis=1)
+    keys = keys * lax.rsqrt(head_means(keys) + EPS) * kgain
+    kv[kvx.slot(c, ln, g)] = jnp.concatenate([keys, kv_raw[:, kdim:]], axis=1).astype(BF16)
 
     pl.semaphore_wait(barrier, 7)
-
-    @each(4, 1)
-    def _(k):
-        gather_copy(k).start()
-
-    @each(4, 1)
-    def _(k):
-        line_copy(g, k).start()
-
-    pair_copy(g, ln).start()
-
+    kvx.send_own()
+
+    qgain = jnp.concatenate([qgain_ref[...] * (HEAD**-0.5 * math.log2(math.e))] * 4, axis=1)
     low_half = lax.broadcasted_iota(jnp.int32, (tok, 128), 1) < HEAD
     for t in range(QH * HEAD // 256):
         part = attn_in[:, 256 * t : 256 * t + 256].astype(F32)
-        query = part * lax.rsqrt(head_means(part) + EPS) * qgain_ref[:, 256 * t : 256 * t + 256]
+        query = part * lax.rsqrt(head_means(part) + EPS) * qgain
         for n in range(4):
             head = 4 * t + n
             at = (head // group) % 2
@@ -142,114 +225,127 @@
             tile = jnp.where(low_half == (at == 0), tile, 0.0)
             first = head % group * tok
             qs[head // group, first : first + tok, :] = tile.astype(BF16)
-
-    @each(4, 1)
-    def _(k):
-        gp = (g + k) % 4
-        arrival(peer(gp, ln)).wait_recv()
-
-        @each(4, 1)
-        def _(m):
-            line_copy(gp, m).start()
-
-        pair_copy(gp, ln).start()
-
-    @each(4)
-    def _(m):
-        gp = (g + m) % 4
-
-        @each(4, 1)
-        def _(k):
-            lp = (ln + k) % 4
-            arrival(peer(gp, lp)).wait_recv()
-            pair_copy(gp, lp).start()
-
-    @each(16)
-    def _(n):
-        arrival(2 * n + 1 - c).wait_recv()
-
-    span = 4 * tok
+    acc[...] = jnp.zeros_like(acc)
+
+    kvx.take_gathered()
+    if gathers:
+        wx.send_own()
+
     ones = jnp.ones((span, 128), BF16)
-    last = me // 4
-    rows = group * tok
-    qpos = me * tok + lax.broadcasted_iota(jnp.int32, (rows, span), 0) % tok
-    upos = lax.broadcasted_iota(jnp.int32, (rows, span), 1)
-
-    @each(KVH // 2)
-    def _(pair):
-        kcols = pl.ds(pl.multiple_of(pair * 128, 128), 128)
-        vcols = pl.ds(pl.multiple_of(kdim + pair * 128, 128), 128)
-        for at in range(2):
-
-            def step(kb, masked):
-                keys = kv[pl.ds(4 * kb, 4), :, kcols].reshape(span, 128)
-                values = kv[pl.ds(4 * kb, 4), :, vcols].reshape(span, 128)
+    qpos = me * tok + lax.broadcasted_iota(jnp.int32, (rows, 1), 0) % tok
+    unit = lax.broadcasted_iota(jnp.int32, (1, span), 1)
+
+    def attend_to(t, lp):
+        base = t * (8 * lp + 1) + (1 - t) * 2 * lp
+        stride = 2 * t + 8 * (1 - t)
+
+        @pl.when(base <= me)
+        def _():
+            kpos = (base + stride * (unit // tok)) * tok + unit % tok
+
+            @each(KVH)
+            def _(head):
+                kcols = pl.ds(pl.multiple_of(head // 2 * 128, 128), 128)
+                vcols = pl.ds(pl.multiple_of(kdim + head // 2 * 128, 128), 128)
+                blocks = pl.ds((t * 4 + lp) * 4, 4)
+                keys = kv[blocks, :, kcols].reshape(span, 128)
+                values = kv[blocks, :, vcols].reshape(span, 128)
                 score = lax.dot_general(
-                    qs[2 * pair + at],
-                    keys,
-                    (((1,), (1,)), ((), ())),
-                    preferred_element_type=F32,
+                    qs[head], keys, (((1,), (1,)), ((), ())), preferred_element_type=F32
                 )
-                expw = jnp.exp2(score)
-                if masked:
-                    expw = jnp.where(upos + kb * span <= qpos, expw, 0.0)
-                return jnp.dot(
+                expw = jnp.where(kpos <= qpos, jnp.exp2(score), 0.0)
+                acc[head] += jnp.dot(
                     expw.astype(BF16),
                     jnp.concatenate([values, ones], axis=1),
                     preferred_element_type=F32,
                 )
 
-            acc[...] = step(last, True)
-
-            def body(kb, carry):
-                acc[...] += step(kb, False)
-                return carry
-
-            lax.fori_loop(0, last, body, 0)
-            mixed = acc[:, :128] / acc[:, 128:]
-            for n in range(group // 2):
-                even = mixed[2 * n * tok : (2 * n + 1) * tok]
-                odd = mixed[(2 * n + 1) * tok : (2 * n + 2) * tok]
-                if at == 0:
-                    odd = pltpu.roll(odd, HEAD, 1)
-                else:
-                    even = pltpu.roll(even, HEAD, 1)
-                first = pl.multiple_of((2 * pair + at) * (group // 2) * 128 + n * 128, 128)
-                out_ref[:, pl.ds(first, 128)] = jnp.where(low_half, even, odd).astype(BF16)
-
-    @each(4, 1)
-    def _(k):
-        gather_copy(k).wait_send()
-
     @each(4)
-    def _(gp):
-        @each(4, 1)
-        def _(k):
-            line_copy(gp, k).wait_send()
+    def _(q):
+        by = q + q // 2 - 2 * (q // 3)
+
+        @pl.when(q > 0)
+        def _():
+            kvx.take_line(by)
+
+        attend_to(c, (ln + by) % 4)
+        if gathers:
+
+            @pl.when(q == 1)
+            def _():
+                wx.take_gathered()
+
+            @pl.when(q == 3)
+            def _():
+                wx.take_line(1)
+                wx.take_line(3)
+
+        kvx.take_pair((g + by) % 4)
+        attend_to(1 - c, (g + by) % 4)
+
+    def mixed(head, offset):
+        at = pl.ds(offset * tok, tok)
+        return acc[head, at, :128] / acc[head, at, 128:]
+
+    for lp in range(4):
+        for gp in (0, 2):
+            first = (2 * lp + gp // 2) * 128
+            tile = jnp.where(low_half, mixed(gp, 2 * lp), mixed(gp + 1, 2 * lp))
+            att[:, first : first + 128] = tile.astype(BF16)
+            one, two = mixed(lp, 2 * gp + 1), mixed(lp, 2 * gp + 3)
+            if lp % 2 == 0:
+                two = pltpu.roll(two, HEAD, 1)
+            else:
+                one = pltpu.roll(one, HEAD, 1)
+            att[:, 1024 + first : 1024 + first + 128] = jnp.where(low_half, one, two).astype(BF16)
+
+    if gathers:
+        wx.take_line(2)
 
         @each(4)
         def _(lp):
-            pair_copy(gp, lp).wait_send()
-
-
-def attend(hidden, attn_gain, q_gain, k_gain, kv_w, tick):
+            wx.take_pair(lp)
+
+        keep.start()
+    else:
+        fetch.wait()
+
+    for n in range(h_ref.shape[1] // 256):
+        cols = slice(n * 256, n * 256 + 256)
+        made = jnp.dot(
+            att[...], wf[:, :, cols].reshape(QH * HEAD, 256), preferred_element_type=F32
+        )
+        after_ref[:, cols] = h_ref[:, cols].astype(F32) + made
+
+    kvx.finish()
+    if gathers:
+        wx.finish()
+        keep.wait()
+
+
+def attend(hidden, attn_gain, q_gain, k_gain, kv_w, w, tick):
     tok, d = hidden.shape
     vmem = pl.BlockSpec(memory_space=pltpu.VMEM)
+    hbm = pl.BlockSpec(memory_space=pl.ANY)
     dma = pltpu.SemaphoreType.DMA
-    qscale = jnp.tile(q_gain * (HEAD**-0.5 * math.log2(math.e)), QH)[None]
+    gathers = tick == 0
+    after = jax.ShapeDtypeStruct((tok, d), F32)
+    whole = jax.ShapeDtypeStruct((32, HEAD, d), BF16)
+    sems = [dma((4,)), dma((8,)), dma((4,)), dma((16,)), dma((32,))]
     return pl.pallas_call(
-        attn_kernel,
-        out_shape=jax.ShapeDtypeStruct((tok, d), BF16),
-        in_specs=[vmem] * 5,
-        out_specs=vmem,
+        functools.partial(attn_kernel, gathers),
+        out_shape=[after, whole] if gathers else [after],
+        in_specs=[vmem] * 5 + [vmem if gathers else hbm],
+        out_specs=[vmem, hbm] if gathers else [vmem],
         scratch_shapes=[
             pltpu.VMEM((32, tok, 2 * KVH * HEAD), BF16),
             pltpu.VMEM((KVH, QH // KVH * tok, 128), BF16),
-            pltpu.VMEM((QH // KVH * tok, 256), F32),
-            dma((4,)),
-            dma((16,)),
-            dma((16,)),
-            dma((32,)),
+            pltpu.VMEM((KVH, QH // KVH * tok, 256), F32),
+            pltpu.VMEM((tok, d), BF16),
+            pltpu.VMEM((32, HEAD, d), BF16),
+            dma,
+            *sems,
+            *(sems if gathers else []),
         ],
         compiler_params=pltpu.CompilerParams(
             collective_id=2 + tick, has_side_effects=True, vmem_limit_bytes=56 << 20
@@ -257,7 +353,7 @@
         cost_estimate=pl.CostEstimate(
             flops=40 * 10**9, bytes_accessed=20 * 10**6, transcendentals=10**6
         ),
-    )(hidden, attn_gain[None], qscale, jnp.tile(k_gain, KVH)[None], kv_w)
+    )(hidden, attn_gain, q_gain, k_gain, kv_w, w)
 
 
 def moe_kernel(
@@ -266,12 +362,13 @@
     *refs,
 ):
     if passes:
-        x_ref, after_ref, info_ref, gu_hbm, dn_hbm, fresh_ref, out_ref, next_ref = refs[:8]
+        after_ref, gain_ref, ids_ref, gates_ref, gu_hbm, dn_hbm, fresh_ref = refs[:7]
+        out_ref, next_ref = refs[7:9]
         ob, nb, s5, r5 = refs[-4:]
-        refs = refs[8:-4]
+        refs = refs[9:-4]
     else:
-        x_ref, after_ref, info_ref, gu_hbm, dn_hbm, out_ref = refs[:6]
-        refs = refs[6:]
+        after_ref, gain_ref, ids_ref, gates_ref, gu_hbm, dn_hbm, out_ref = refs[:7]
+        refs = refs[7:]
     (
     xg,
     sb,
@@ -406,9 +503,13 @@
                 barrier, inc=1, device_id=((sec + by) % 4, me), device_id_type=MESH
             )
 
-    infog[g] = info_ref[...]
+    gates = gates_ref[...].astype(F32) * (1.0 / 1024.0)
+    infog[g] = route_info(ids_ref[...], gates, 64)
+    after = after_ref[...]
+    scale = lax.rsqrt(jnp.mean(after * after, axis=-1, keepdims=True) + EPS)
     for j in range(chunks):
-        xg[j, g] = x_ref[:, j * width : (j + 1) * width]
+        cols = slice(j * width, (j + 1) * width)
+        xg[j, g] = (after_ref[:, cols] * scale * gain_ref[:, cols]).astype(BF16)
     pl.semaphore_wait(barrier, 15 if passes else 13)
 
     @each(4, 1)
@@ -501,7 +602,7 @@
         @each(640 // 128)
         def _(m):
             at = pl.ds(pl.multiple_of(m * 128, 128), 128)
-            hid[e, at, :] = (jax.nn.silu(acc[e, at, :ff]) * acc[e, at, ff:]).astype(BF16)
+            hid[e, at, :] = (silu(acc[e, at, :ff]) * acc[e, at, ff:]).astype(BF16)
 
     dn_copy.wait()
 
@@ -588,8 +689,8 @@
             back_copy(j, (my_slot + k) % 8).wait_send()
 
 
-def moe_layer(moe_in, after_attn, info, gate_up, down, cap, tick, fresh):
-    tok, d = moe_in.shape
+def moe_layer(after_attn, gain, ids, gates, gate_up, down, cap, tick, fresh):
+    tok, d = after_attn.shape
     ff = down.shape[1]
     w = d // CHUNKS
     rows = 8 * cap
@@ -607,7 +708,7 @@
     return pl.pallas_call(
         functools.partial(moe_kernel, cap, passes),
         out_shape=[jax.ShapeDtypeStruct((tok, d), BF16)] * outs,
-        in_specs=[vmem, vmem, vmem, hbm, hbm] + [vmem] * passes,
+        in_specs=[vmem] * 4 + [hbm, hbm] + [vmem] * passes,
         out_specs=[vmem] * outs,
         scratch_shapes=[
             pltpu.VMEM((CHUNKS, 4, tok, w), BF16),
@@ -645,7 +746,7 @@
         cost_estimate=pl.CostEstimate(
             flops=12 * 10**9, bytes_accessed=20 * 10**6, transcendentals=10**6
         ),
-    )(moe_in, after_attn, info, gate_up, down, *([fresh] if passes else []))
+    )(after_attn, gain, ids.T, gates.T, gate_up, down, *([fresh] if passes else []))
 
 
 def body(
@@ -666,20 +767,24 @@
     tok = section_input.shape[1]
     experts_all = expert_gate_up.shape[1] * devices
     cap = tok * TOPK * 9 // (8 * experts_all)
-    infos = [route_info(route_ids[0, t], route_weights[0, t], experts_all) for t in range(2)]
-    out_full = lax.all_gather(out_weight[0], "expert", axis=0, tiled=True)
-
-    def layer(hidden, tick, fresh):
-        h32 = hidden.astype(F32)
-        attended = attend(hidden, attn_gain[0], query_gain[0], key_gain[0], kv_weight[0], tick)
-        after_attn = h32 + jnp.dot(attended, out_full, preferred_element_type=F32)
-        moe_in = rms_scale(after_attn, moe_gain[0]).astype(BF16)
-        return moe_layer(
-            moe_in, after_attn, infos[tick], expert_gate_up[0], expert_down[0], cap, tick, fresh
+
+    def layer(hidden, tick, w, fresh):
+        after_attn, *w = attend(hidden, attn_gain, query_gain, key_gain, kv_weight[0], w, tick)
+        outs = moe_layer(
+            after_attn,
+            moe_gain,
+            route_ids[0, tick],
+            route_weights[0, tick],
+            expert_gate_up[0],
+            expert_down[0],
+            cap,
+            tick,
+            fresh,
         )
-
-    first_out, second_in = layer(section_input[0], 0, fresh_batch)
-    (second_out,) = layer(second_in, 1, None)
+        return outs, w
+
+    (first_out, second_in), (out_full,) = layer(section_input[0], 0, out_weight[0], fresh_batch)
+    (second_out,), _ = layer(second_in, 1, out_full, None)
     return (first_out[None], second_out[None])
 
 

time: 343 us -> 301 us (0.88)
  waiting for transfers between devices: 21.4 us -> 0 us
  between operations: 14.1 us -> 0.66 us
  Pallas kernels: 281 us -> 293 us
  matrix products: 10.3 us -> 0 us
  other arithmetic: 4.72 us -> 0 us
    pallas_call x2, Pallas kernels: 61.4 us -> 89 us  [attend(): pl.pallas_call(functools.partial(attn_kernel, gathers), out_shape=[after,...]
    all_gather x1 -> x0, waiting for transfers between devices: 20.7 us -> none  [body(): out_full = lax.all_gather(out_weight[0], 'expert', axis=0, tiled=True)]
    pallas_call x2, Pallas kernels: 220 us -> 204 us  [moe_layer(): pl.pallas_call(functools.partial(moe_kernel, cap, passes), out_shape=[jax...]
    dot_general x4 -> x0, matrix products: 10.3 us -> none  [the longest x2 9.92 us: layer(): after_attn = h32 + jnp.dot(attended, out_full, preferred_element_type=F32)]
  transfers between devices with their start and end apart: 1 -> 0, of which waited for: 1 -> 0; matrix products, arithmetic and copies ran while one was open for 2% -> 0% of each run, Pallas kernels for 10% -> 0%
where the time goes in v3:
time: 301 us; the launch traced here: 299 us
  Pallas kernels  293 us (97%)
  local copies, waits for them, and re-layouts  5.11 us (2%)
    pallas_call x2, Pallas kernels, moe_layer(): pl.pallas_call(functools.partial(moe_kernel, cap, passes), out_shape=[jax...  204 us
    pallas_call x2, Pallas kernels, attend(): pl.pallas_call(functools.partial(attn_kernel, gathers), out_shape=[after,...  89 us

profile of v3, /device:TPU:32, one launch (start us, length us, event | category | flops | bytes accessed | tf_op | source)
XLA Modules:
  0.0 299.0 jit_solution(16446411491693300755)
XLA Ops:
  0.6 1.3 slice_bitcast_fusion
  2.0 56.3 %shard_map.131 = (f32[128,2048]{1,0:T(8,128)}, bf16[32,64,2048]{2,1,0:T(8,128)(2,1)}) custom-call(bf16[128,2048]{1,0:T(8,128)(2,1)} %bitcast.31, f32[1,2048]{1,0:T(1,128)} %refs_1_.6, f32[1,64]{1,0:T(1,128)} %refs_2_.3, f32[1,64]{1,0:T(1,128)} %refs_3_.3, bf16[2048,512]{1,0:T(8,128)(2,1)} %bitcast.29, bf16[64,2048]{1,0:T(8,128)(2,1)} %bitcast.32), custom_call_target="tpu_custom_call" | custom-call | flops 40000000000 | bytes 20000000 | tf_op jit(solution)/shard_map/pallas_call | solution.py:335
  58.3 103.0 %shard_map.132 = (bf16[128,2048]{1,0:T(8,128)(2,1)}, bf16[128,2048]{1,0:T(8,128)(2,1)}) custom-call(f32[128,2048]{1,0:T(8,128)} %get-tuple-element.6.refs_0_, f32[1,2048]{1,0:T(1,128)} %refs_1_.7, s32[8,128]{1,0:T(8,128)} %get-tuple-element.14.refs_2_, s32[8,128]{1,0:T(8,128)} %get-tuple-element.11.refs_3_, bf16[2,2048,1536]{2,1,0:T(8,128)(2,1)} %bitcast.25, ...), custom_call_target="tpu_custom_call" | custom-call | flops 12000000000 | bytes 20000000 | tf_op jit(solution)/shard_map/pallas_call | solution.py:708
  161.3 32.7 %shard_map.133.refs_0_ = f32[128,2048]{1,0:T(8,128)} custom-call(bf16[128,2048]{1,0:T(8,128)(2,1)} %get-tuple-element.8.refs_0_, f32[1,2048]{1,0:T(1,128)} %refs_1_.6, f32[1,64]{1,0:T(1,128)} %refs_2_.3, f32[1,64]{1,0:T(1,128)} %refs_3_.3, bf16[2048,512]{1,0:T(8,128)(2,1)} %bitcast.30, bf16[32,64,2048]{2,1,0:T(8,128)(2,1)} %get-tuple-element.9.refs_5_), custom_call_target="tpu_custom_call" | custom-call | flops 40000000000 | bytes 20000000 | tf_op jit(solution)/shard_map/pallas_call | solution.py:335
  193.9 101.3 %shard_map.134 = bf16[128,2048]{1,0:T(8,128)(2,1)} custom-call(f32[128,2048]{1,0:T(8,128)} %shard_map.133.refs_0_, f32[1,2048]{1,0:T(1,128)} %refs_1_.7, s32[8,128]{1,0:T(8,128)} %get-tuple-element.15.refs_2_, s32[8,128]{1,0:T(8,128)} %get-tuple-element.10.refs_3_, bf16[2,2048,1536]{2,1,0:T(8,128)(2,1)} %bitcast.26, bf16[2,768,2048]{2,1,0:T(8,128)(2,1)} %bitcast.28), custom_call_target="tpu_custom_call" | custom-call | flops 12000000000 | bytes 20000000 | tf_op jit(solution)/shard_map/pallas_call | solution.py:708
  295.3 1.9 copy.16
  297.1 1.9 copy.17

commit v4 on v3

--- a/solution.py
+++ b/solution.py
@@ -187,6 +187,10 @@
         fetch = pltpu.make_async_copy(w_ref, wf, wsem)
         fetch.start()
 
+    pl.semaphore_wait(barrier, 7)
+    if gathers:
+        wx.send_own()
+
     r0 = lax.broadcasted_iota(jnp.int32, (256, 256), 0) // HEAD
     c0 = lax.broadcasted_iota(jnp.int32, (256, 256), 1) // HEAD
     averager = jnp.where(r0 == c0, 1.0 / HEAD, 0.0).astype(BF16)
@@ -208,7 +212,6 @@
     keys = keys * lax.rsqrt(head_means(keys) + EPS) * kgain
     kv[kvx.slot(c, ln, g)] = jnp.concatenate([keys, kv_raw[:, kdim:]], axis=1).astype(BF16)
 
-    pl.semaphore_wait(barrier, 7)
     kvx.send_own()
 
     qgain = jnp.concatenate([qgain_ref[...] * (HEAD**-0.5 * math.log2(math.e))] * 4, axis=1)
@@ -229,9 +232,8 @@
 
     kvx.take_gathered()
     if gathers:
-        wx.send_own()
-
-    ones = jnp.ones((span, 128), BF16)
+        wx.take_gathered()
+
     qpos = me * tok + lax.broadcasted_iota(jnp.int32, (rows, 1), 0) % tok
     unit = lax.broadcasted_iota(jnp.int32, (1, span), 1)
 
@@ -250,13 +252,15 @@
                 blocks = pl.ds((t * 4 + lp) * 4, 4)
                 keys = kv[blocks, :, kcols].reshape(span, 128)
                 values = kv[blocks, :, vcols].reshape(span, 128)
+                own = (lax.broadcasted_iota(jnp.int32, (span, 128), 1) // HEAD) == head % 2
+                value = jnp.where(own, values.astype(F32), 1.0).astype(BF16)
                 score = lax.dot_general(
                     qs[head], keys, (((1,), (1,)), ((), ())), preferred_element_type=F32
                 )
                 expw = jnp.where(kpos <= qpos, jnp.exp2(score), 0.0)
                 acc[head] += jnp.dot(
                     expw.astype(BF16),
-                    jnp.concatenate([values, ones], axis=1),
+                    value,
                     preferred_element_type=F32,
                 )
 
@@ -264,40 +268,38 @@
     def _(q):
         by = q + q // 2 - 2 * (q // 3)
 
-        @pl.when(q > 0)
-        def _():
-            kvx.take_line(by)
-
-        attend_to(c, (ln + by) % 4)
         if gathers:
-
-            @pl.when(q == 1)
-            def _():
-                wx.take_gathered()
 
             @pl.when(q == 3)
             def _():
                 wx.take_line(1)
                 wx.take_line(3)
 
+        @pl.when(q > 0)
+        def _():
+            kvx.take_line(by)
+
+        attend_to(c, (ln + by) % 4)
         kvx.take_pair((g + by) % 4)
         attend_to(1 - c, (g + by) % 4)
 
     def mixed(head, offset):
         at = pl.ds(offset * tok, tok)
-        return acc[head, at, :128] / acc[head, at, 128:]
+        both = acc[head, at, :]
+        return both / pltpu.roll(both, HEAD, 1)
 
     for lp in range(4):
         for gp in (0, 2):
-            first = (2 * lp + gp // 2) * 128
+            cols = slice((4 * lp + gp) * HEAD, (4 * lp + gp) * HEAD + 128)
+            far = slice(1024 + cols.start, 1024 + cols.stop)
             tile = jnp.where(low_half, mixed(gp, 2 * lp), mixed(gp + 1, 2 * lp))
-            att[:, first : first + 128] = tile.astype(BF16)
+            att[:, cols] = tile.astype(BF16)
             one, two = mixed(lp, 2 * gp + 1), mixed(lp, 2 * gp + 3)
             if lp % 2 == 0:
                 two = pltpu.roll(two, HEAD, 1)
             else:
                 one = pltpu.roll(one, HEAD, 1)
-            att[:, 1024 + first : 1024 + first + 128] = jnp.where(low_half, one, two).astype(BF16)
+            att[:, far] = jnp.where(low_half, one, two).astype(BF16)
 
     if gathers:
         wx.take_line(2)
@@ -340,7 +342,7 @@
         scratch_shapes=[
             pltpu.VMEM((32, tok, 2 * KVH * HEAD), BF16),
             pltpu.VMEM((KVH, QH // KVH * tok, 128), BF16),
-            pltpu.VMEM((KVH, QH // KVH * tok, 256), F32),
+            pltpu.VMEM((KVH, QH // KVH * tok, 128), F32),
             pltpu.VMEM((tok, d), BF16),
             pltpu.VMEM((32, HEAD, d), BF16),
             dma,
@@ -358,6 +360,7 @@
 
 def moe_kernel(
     cap,
+    tick,
     passes,
     *refs,
 ):
@@ -503,8 +506,8 @@
                 barrier, inc=1, device_id=((sec + by) % 4, me), device_id_type=MESH
             )
 
-    gates = gates_ref[...].astype(F32) * (1.0 / 1024.0)
-    infog[g] = route_info(ids_ref[...], gates, 64)
+    gates = gates_ref[tick].astype(F32) * (1.0 / 1024.0)
+    infog[g] = route_info(ids_ref[tick], gates, 64)
     after = after_ref[...]
     scale = lax.rsqrt(jnp.mean(after * after, axis=-1, keepdims=True) + EPS)
     for j in range(chunks):
@@ -524,8 +527,6 @@
 
     gu_copy.start()
     dn_copy.start()
-    acc[...] = jnp.zeros_like(acc)
-
     row = lax.broadcasted_iota(jnp.int32, (half, 512), 0)
     lane = lax.broadcasted_iota(jnp.int32, (half, 512), 1)
     block_of_row = (
@@ -539,20 +540,16 @@
     def _(k):
         info_arrival(k).wait_recv()
 
+    def hits(i, e):
+        at = 2 * line_dev(i) + e
+        rank = jnp.concatenate([infog[b, pl.ds(at, 1), :] for b in range(4)], axis=1)
+        return rank == pattern
+
     @each(8)
     def _(i):
-        dev = line_dev(i)
-        picks, gates = [], []
-        for e in range(2):
-            at = 2 * dev + e
-            rank = jnp.concatenate([infog[b, pl.ds(at, 1), :] for b in range(4)], axis=1)
-            gate = jnp.concatenate([infog[b, pl.ds(64 + at, 1), :] for b in range(4)], axis=1)
-            hit = rank == pattern
-            picks.append(jnp.where(hit, 1.0, 0.0))
-            gates.append(jnp.where(hit, gate, 0.0))
+        picks = [jnp.where(hits(i, e), 1.0, 0.0) for e in range(2)]
         at = pl.multiple_of(i * rows, 16)
         sel[pl.ds(at, rows), :] = jnp.concatenate(picks, axis=0).astype(BF16)
-        cw[pl.ds(at, rows), :] = jnp.concatenate(gates, axis=0).astype(BF16)
 
     @each(chunks)
     def _(j):
@@ -573,11 +570,22 @@
 
         xb[j, my_slot] = sb[j, my_line]
 
+    @each(8)
+    def _(i):
+        gates = []
+        for e in range(2):
+            at = 64 + 2 * line_dev(i) + e
+            gate = jnp.concatenate([infog[b, pl.ds(at, 1), :] for b in range(4)], axis=1)
+            gates.append(jnp.where(hits(i, e), gate, 0.0))
+        at = pl.multiple_of(i * rows, 16)
+        cw[pl.ds(at, rows), :] = jnp.concatenate(gates, axis=0).astype(BF16)
+
     for m in range(8 * rows // 128):
         ct[:, m * 128 : (m + 1) * 128] = (
             cw[m * 128 : (m + 1) * 128, :].astype(F32).T.astype(BF16)
         )
 
+    acc[...] = jnp.zeros_like(acc)
     gu_copy.wait()
 
     @each(chunks)
@@ -706,7 +714,7 @@
         dma((CHUNKS,)),
     ]
     return pl.pallas_call(
-        functools.partial(moe_kernel, cap, passes),
+        functools.partial(moe_kernel, cap, tick, passes),
         out_shape=[jax.ShapeDtypeStruct((tok, d), BF16)] * outs,
         in_specs=[vmem] * 4 + [hbm, hbm] + [vmem] * passes,
         out_specs=[vmem] * outs,
@@ -746,7 +754,7 @@
         cost_estimate=pl.CostEstimate(
             flops=12 * 10**9, bytes_accessed=20 * 10**6, transcendentals=10**6
         ),
-    )(after_attn, gain, ids.T, gates.T, gate_up, down, *([fresh] if passes else []))
+    )(after_attn, gain, ids, gates, gate_up, down, *([fresh] if passes else []))
 
 
 def body(
@@ -773,8 +781,8 @@
         outs = moe_layer(
             after_attn,
             moe_gain,
-            route_ids[0, tick],
-            route_weights[0, tick],
+            route_ids[0].transpose(0, 2, 1),
+            route_weights[0].transpose(0, 2, 1),
             expert_gate_up[0],
             expert_down[0],
             cap,

time: 301 us -> 294 us (0.977)
  Pallas kernels: 293 us -> 288 us
where the time goes in v4:
time: 294 us; the launch traced here: 292 us
  Pallas kernels  288 us (98%)
  local copies, waits for them, and re-layouts  3.76 us (1%)
    pallas_call x2, Pallas kernels, moe_layer(): pl.pallas_call(functools.partial(moe_kernel, cap, tick, passes), out_shap...  201 us
    pallas_call x2, Pallas kernels, attend(): pl.pallas_call(functools.partial(attn_kernel, gathers), out_shape=[after,...  86.4 us

profile of v4, /device:TPU:32, one launch (start us, length us, event | category | flops | bytes accessed | tf_op | source)
XLA Modules:
  0.0 292.3 jit_solution(14472829894400635343)
XLA Ops:
  0.6 53.3 %shard_map.131 = (f32[128,2048]{1,0:T(8,128)}, bf16[32,64,2048]{2,1,0:T(8,128)(2,1)}) custom-call(bf16[128,2048]{1,0:T(8,128)(2,1)} %bitcast.21, f32[1,2048]{1,0:T(1,128)} %refs_1_.6, f32[1,64]{1,0:T(1,128)} %refs_2_.3, f32[1,64]{1,0:T(1,128)} %refs_3_.3, bf16[2048,512]{1,0:T(8,128)(2,1)} %bitcast.19, bf16[64,2048]{1,0:T(8,128)(2,1)} %bitcast.22), custom_call_target="tpu_custom_call" | custom-call | flops 40000000000 | bytes 20000000 | tf_op jit(solution)/shard_map/pallas_call | solution.py:337
  54.0 101.5 %shard_map.132 = (bf16[128,2048]{1,0:T(8,128)(2,1)}, bf16[128,2048]{1,0:T(8,128)(2,1)}) custom-call(f32[128,2048]{1,0:T(8,128)} %get-tuple-element.6.refs_0_, f32[1,2048]{1,0:T(1,128)} %refs_1_.7, s32[2,8,128]{2,1,0:T(8,128)} %bitcast.23, s32[2,8,128]{2,1,0:T(8,128)} %bitcast.25, bf16[2,2048,1536]{2,1,0:T(8,128)(2,1)} %bitcast.15, ...), custom_call_target="tpu_custom_call" | custom-call | flops 12000000000 | bytes 20000000 | tf_op jit(solution)/shard_map/pallas_call | solution.py:716
  155.4 33.1 %shard_map.133.refs_0_ = f32[128,2048]{1,0:T(8,128)} custom-call(bf16[128,2048]{1,0:T(8,128)(2,1)} %get-tuple-element.8.refs_0_, f32[1,2048]{1,0:T(1,128)} %refs_1_.6, f32[1,64]{1,0:T(1,128)} %refs_2_.3, f32[1,64]{1,0:T(1,128)} %refs_3_.3, bf16[2048,512]{1,0:T(8,128)(2,1)} %bitcast.20, bf16[32,64,2048]{2,1,0:T(8,128)(2,1)} %get-tuple-element.9.refs_5_), custom_call_target="tpu_custom_call" | custom-call | flops 40000000000 | bytes 20000000 | tf_op jit(solution)/shard_map/pallas_call | solution.py:337
  188.6 100.0 %shard_map.134 = bf16[128,2048]{1,0:T(8,128)(2,1)} custom-call(f32[128,2048]{1,0:T(8,128)} %shard_map.133.refs_0_, f32[1,2048]{1,0:T(1,128)} %refs_1_.7, s32[2,8,128]{2,1,0:T(8,128)} %bitcast.24, s32[2,8,128]{2,1,0:T(8,128)} %bitcast.26, bf16[2,2048,1536]{2,1,0:T(8,128)(2,1)} %bitcast.16, bf16[2,768,2048]{2,1,0:T(8,128)(2,1)} %bitcast.18), custom_call_target="tpu_custom_call" | custom-call | flops 12000000000 | bytes 20000000 | tf_op jit(solution)/shard_map/pallas_call | solution.py:716
  288.6 1.9 copy.16
  290.5 1.9 copy.17

commit v5 on v4

--- a/solution.py
+++ b/solution.py
@@ -757,6 +757,24 @@
     )(after_attn, gain, ids, gates, gate_up, down, *([fresh] if passes else []))
 
 
+def settle_kernel(first, second, first_out, second_out):
+    first_out[...] = first[...]
+    second_out[...] = second[...]
+
+
+def settle(first, second):
+    vmem = pl.BlockSpec(memory_space=pltpu.VMEM)
+    return pl.pallas_call(
+        settle_kernel,
+        out_shape=(
+            jax.ShapeDtypeStruct(first.shape, first.dtype),
+            jax.ShapeDtypeStruct(second.shape, second.dtype),
+        ),
+        in_specs=[vmem, vmem],
+        out_specs=(vmem, vmem),
+    )(first, second)
+
+
 def body(
     section_input,
     fresh_batch,
@@ -793,7 +811,7 @@
 
     (first_out, second_in), (out_full,) = layer(section_input[0], 0, out_weight[0], fresh_batch)
     (second_out,), _ = layer(second_in, 1, out_full, None)
-    return (first_out[None], second_out[None])
+    return settle(first_out[None], second_out[None])
 
 
 def solution(mesh):

time: 294 us -> 293 us (level)
  local copies, waits for them, and re-layouts: 3.76 us -> 0 us
    unnamed x2 -> x0, local copies, waits for them, and re-layouts: 3.76 us -> none
where the time goes in v5:
time: 293 us; the launch traced here: 291 us
  Pallas kernels  290 us (99%)
    pallas_call x2, Pallas kernels, moe_layer(): pl.pallas_call(functools.partial(moe_kernel, cap, tick, passes), out_shap...  201 us
    pallas_call x2, Pallas kernels, attend(): pl.pallas_call(functools.partial(attn_kernel, gathers), out_shape=[after,...  86.4 us

profile of v5, /device:TPU:32, one launch (start us, length us, event | category | flops | bytes accessed | tf_op | source)
XLA Modules:
  0.0 290.8 jit_solution(4159896119419769469)
XLA Ops:
  0.6 53.3 %shard_map.131 = (f32[128,2048]{1,0:T(8,128)}, bf16[32,64,2048]{2,1,0:T(8,128)(2,1)}) custom-call(bf16[128,2048]{1,0:T(8,128)(2,1)} %bitcast.21, f32[1,2048]{1,0:T(1,128)} %refs_1_.6, f32[1,64]{1,0:T(1,128)} %refs_2_.3, f32[1,64]{1,0:T(1,128)} %refs_3_.3, bf16[2048,512]{1,0:T(8,128)(2,1)} %bitcast.19, bf16[64,2048]{1,0:T(8,128)(2,1)} %bitcast.22), custom_call_target="tpu_custom_call" | custom-call | flops 40000000000 | bytes 20000000 | tf_op jit(solution)/shard_map/pallas_call | solution.py:337
  54.0 101.5 %shard_map.132 = (bf16[128,2048]{1,0:T(8,128)(2,1)}, bf16[128,2048]{1,0:T(8,128)(2,1)}) custom-call(f32[128,2048]{1,0:T(8,128)} %get-tuple-element.6.refs_0_, f32[1,2048]{1,0:T(1,128)} %refs_1_.7, s32[2,8,128]{2,1,0:T(8,128)} %bitcast.23, s32[2,8,128]{2,1,0:T(8,128)} %bitcast.25, bf16[2,2048,1536]{2,1,0:T(8,128)(2,1)} %bitcast.15, ...), custom_call_target="tpu_custom_call" | custom-call | flops 12000000000 | bytes 20000000 | tf_op jit(solution)/shard_map/pallas_call | solution.py:716
  155.4 33.1 %shard_map.133.refs_0_ = f32[128,2048]{1,0:T(8,128)} custom-call(bf16[128,2048]{1,0:T(8,128)(2,1)} %get-tuple-element.8.refs_0_, f32[1,2048]{1,0:T(1,128)} %refs_1_.6, f32[1,64]{1,0:T(1,128)} %refs_2_.3, f32[1,64]{1,0:T(1,128)} %refs_3_.3, bf16[2048,512]{1,0:T(8,128)(2,1)} %bitcast.20, bf16[32,64,2048]{2,1,0:T(8,128)(2,1)} %get-tuple-element.9.refs_5_), custom_call_target="tpu_custom_call" | custom-call | flops 40000000000 | bytes 20000000 | tf_op jit(solution)/shard_map/pallas_call | solution.py:337
  188.6 100.0 %shard_map.134 = bf16[128,2048]{1,0:T(8,128)(2,1)} custom-call(f32[128,2048]{1,0:T(8,128)} %shard_map.133.refs_0_, f32[1,2048]{1,0:T(1,128)} %refs_1_.7, s32[2,8,128]{2,1,0:T(8,128)} %bitcast.24, s32[2,8,128]{2,1,0:T(8,128)} %bitcast.26, bf16[2,2048,1536]{2,1,0:T(8,128)(2,1)} %bitcast.16, bf16[2,768,2048]{2,1,0:T(8,128)(2,1)} %bitcast.18), custom_call_target="tpu_custom_call" | custom-call | flops 12000000000 | bytes 20000000 | tf_op jit(solution)/shard_map/pallas_call | solution.py:716
  288.6 2.2 shard_map.135
